TPU v7x, 256 devices: a whole 4x4x8 slice. The times are simulated.
256 devices in a mesh: rep: 32 (over x_lo, z, core), fsdp: 8 (over x_hi, y).
Axes of the slice: x: 4 (x_hi: 2, x_lo: 2; x = x_hi * 2 + x_lo), y: 4, z: 8, core: 2. Of those that a mesh axis runs over, the one named last changes fastest.
Arguments:
- global_params: bfloat16 [8192, 1024], P('fsdp'), may hold values from -0.0625 to 0.0625
- first_moment: bfloat16 [32, 8192, 1024], P('rep', 'fsdp'), may hold values from -0.19921875 to 0.19921875
- second_moment: bfloat16 [32, 8192, 1024], P('rep', 'fsdp'), may hold values from 9.9658966e-05 to 0.0039978027
- batch: bfloat16 [32, 2, 1024, 8192], P('rep', None, 'fsdp'), may hold values from -6 to 6
- labels: int32 [32, 2, 1024], P('rep', None, 'fsdp'), may hold values from 0 to 1023
- momentum: float32 [8192, 1024], P(('fsdp', 'rep')), may hold values from -0.3 to 0.3
- left_root: bfloat16 [8192, 1024], P(('fsdp', 'rep')), may hold values from -4 to 3
- right_root: bfloat16 [8, 1024, 1024], P('fsdp', 'rep'), may hold values from -4 to 3
Outputs:
- new_params: bfloat16 [8192, 1024], P('fsdp')
- new_momentum: float32 [8192, 1024], P(('fsdp', 'rep'))
All inputs are finite; a program needn't handle non-finite values.
Results may differ from a plain program's by a relative error of at most 0.0075.
Values may be sent and summed in bfloat16 or wider, within the bound.
No kernel may reach another device: no remote copies, remote signals or barrier semaphores. Data moves between devices by JAX's collectives and lax.ppermute only.
A program may use at most 128 MiB of HBM per device.

v0:
```python
import jax
import jax.numpy as jnp
from jax import lax
from jax.sharding import PartitionSpec as P

INNER = 2


inner_rate = 0.01
beta_one = 0.9
beta_two = 0.95
adam_eps = 1e-08
decay_rate = 0.1
outer_rate = 0.7
outer_mom = 0.9


def shards(
    global_params, first_moment, second_moment, batch, labels, momentum, left_root, right_root
):
    shard_rows = global_params.shape[0]
    out_width = global_params.shape[1]
    block_rows = left_root.shape[1]
    tok_rows = batch.shape[2]
    groups = lax.axis_size("fsdp")
    weights = global_params.astype(jnp.float32)
    moment_one = first_moment[0].astype(jnp.float32)
    moment_two = second_moment[0].astype(jnp.float32)
    columns = jnp.arange(out_width, dtype=jnp.int32)
    total_tokens = tok_rows * groups
    for step in range(INNER):
        rounded = weights.astype(jnp.bfloat16)
        target = (labels[0, step][:, None] == columns[None, :]).astype(jnp.float32)
        features = batch[0, step]
        projected = jnp.dot(
            features,
            lax.all_gather(rounded, "fsdp", axis=0, tiled=True),
            preferred_element_type=jnp.float32,
        )
        residual_grad = ((projected - target) / total_tokens).astype(jnp.bfloat16)
        grad = lax.psum_scatter(
            lax.dot_general(
                features,
                residual_grad,
                (((0,), (0,)), ((), ())),
                preferred_element_type=jnp.float32,
            ).astype(jnp.bfloat16),
            "fsdp",
            scatter_dimension=0,
            tiled=True,
        ).astype(jnp.float32)
        count = step + 1
        moment_one = beta_one * moment_one + (1.0 - beta_one) * grad
        moment_two = beta_two * moment_two + (1.0 - beta_two) * grad * grad
        corrected_one = moment_one / (1.0 - beta_one**count)
        corrected_two = moment_two / (1.0 - beta_two**count)
        weights = weights - inner_rate * (
            corrected_one / (jnp.sqrt(corrected_two) + adam_eps) + decay_rate * weights
        )
    change = global_params.astype(jnp.float32) - weights
    replicas = lax.axis_size("rep")
    owned = shard_rows // replicas
    first_row = lax.axis_index("rep") * owned
    block_index = first_row // block_rows
    right_full = lax.all_gather(right_root, "rep", axis=1, tiled=True)
    total = lax.psum(change, "rep")
    averaged = total / replicas
    blocks = averaged.reshape(shard_rows // block_rows, block_rows, out_width)
    right_part = jnp.einsum(
        "bik,bkj->bij", blocks, right_full.astype(jnp.float32), precision=lax.Precision.HIGHEST
    )
    block_part = lax.dynamic_index_in_dim(right_part, block_index, 0, keepdims=False)
    precond = jnp.dot(left_root.astype(jnp.float32), block_part, precision=lax.Precision.HIGHEST)
    new_momentum = outer_mom * momentum + precond
    own_params = lax.dynamic_slice_in_dim(global_params, first_row, owned, 0).astype(jnp.float32)
    own_new = (own_params - outer_rate * (precond + outer_mom * new_momentum)).astype(jnp.bfloat16)
    new_params = lax.all_gather(own_new, "rep", axis=0, tiled=True)
    return (new_params, new_momentum)


def solution(mesh):
    in_specs = (
        P("fsdp", None),
        P("rep", "fsdp", None),
        P("rep", "fsdp", None),
        P("rep", None, "fsdp", None),
        P("rep", None, "fsdp"),
        P(("fsdp", "rep"), None),
        P(("fsdp", "rep"), None),
        P("fsdp", "rep", None),
    )
    out_specs = (P("fsdp", None), P(("fsdp", "rep"), None))
    return jax.shard_map(shards, mesh=mesh, in_specs=in_specs, out_specs=out_specs, check_vma=False)
```

profile of v0, /device:TPU:1, one launch (start us, length us, event | category | flops | bytes accessed | tf_op | source)
XLA Modules:
  0.0 1172.9 jit_solution(17665326983349942652)
XLA Ops:
  8.0 0.0 all-gather.5.cloned.1.call-start
  8.1 0.7 all-gather.5.cloned.1.call-update
  8.7 0.0 reduce-scatter.3.cloned.1.call-start
  8.8 0.8 slice_bitcast_fusion
  9.6 193.2 %all-gather.5.cloned.1.call-done = bf16[8192,1024]{1,0:T(8,128)(2,1)} async-done(((bf16[1024,1024]{1,0:T(8,128)(2,1)}), bf16[8192,1024]{1,0:T(8,128)(2,1)}) %all-gather.5.cloned.1.call-update) | async-done | bytes 16777232 | tf_op jit(solution)/shard_map/all_gather | solution.py:37
  202.7 17.5 %convert_bitcast_fusion.1 = bf16[8192,1024]{0,1:T(8,128)(2,1)} fusion(bf16[1,2,128,8192]{3,2,1,0:T(8,128)(2,1)} %param.11, bf16[8192,1024]{1,0:T(8,128)(2,1)} %all-gather.5.cloned.1.call-done, s32[128]{0:T(128)S(1)} %get-tuple-element.5), kind=kOutput, calls=%fused_computation.1 | convolution fusion | flops 4304011264 | bytes 37749248 | tf_op jit(solution)/shard_map/dot_general | solution.py:42
  220.3 0.0 reduce-scatter.3.cloned.1.call-update
  220.3 0.0 all-gather.7.cloned.1.call-start
  220.3 2.9 copy.10
  223.2 4.0 copy.11
  227.2 3.9 copy.12
  231.1 182.8 %reduce-scatter.3.cloned.1.call-done = bf16[1024,1024]{0,1:T(8,128)(2,1)} async-done(((bf16[8192,1024]{0,1:T(8,128)(2,1)}), bf16[1024,1024]{0,1:T(8,128)(2,1)}) %reduce-scatter.3.cloned.1.call-update) | async-done | bytes 2097168 | tf_op jit(solution)/shard_map/reduce_scatter | solution.py:41
  413.9 6.8 fusion.49
  420.7 0.0 all-gather.7.cloned.1.call-update
  420.7 0.2 reduce-scatter.5.cloned.1.call-start
  420.9 189.9 %all-gather.7.cloned.1.call-done = bf16[8192,1024]{0,1:T(8,128)(2,1)} async-done(((bf16[1024,1024]{0,1:T(8,128)(2,1)}), bf16[8192,1024]{0,1:T(8,128)(2,1)}) %all-gather.7.cloned.1.call-update) | async-done | bytes 16777232 | tf_op jit(solution)/shard_map/all_gather | solution.py:37
  610.8 30.9 %convert_bitcast_fusion = bf16[8192,1024]{0,1:T(8,128)(2,1)} fusion(bf16[1,2,128,8192]{3,2,1,0:T(8,128)(2,1)} %param.11, bf16[8192,1024]{0,1:T(8,128)(2,1)} %all-gather.7.cloned.1.call-done, s32[128]{0:T(128)S(1)} %get-tuple-element.4), kind=kOutput, calls=%fused_computation | convolution fusion | flops 4304011264 | bytes 37749248 | tf_op jit(solution)/shard_map/dot_general | solution.py:42
  641.7 0.0 reduce-scatter.5.cloned.1.call-update
  641.7 0.0 all-gather.9.cloned.1.call-start
  641.8 0.5 all-gather.9.cloned.1.call-update
  642.3 0.0 all-reduce.2.cloned.1.call-start
  642.4 196.2 %reduce-scatter.5.cloned.1.call-done = bf16[1024,1024]{0,1:T(8,128)(2,1)} async-done(((bf16[8192,1024]{0,1:T(8,128)(2,1)}), bf16[1024,1024]{0,1:T(8,128)(2,1)}) %reduce-scatter.5.cloned.1.call-update) | async-done | bytes 2097168 | tf_op jit(solution)/shard_map/reduce_scatter | solution.py:41
  838.6 10.6 convert_subtract_fusion
  849.1 0.0 all-reduce.2.cloned.1.call-update
  849.2 0.3 all-gather.11.cloned.1.call-start
  849.5 0.0 all-gather.9.cloned.1.call-done
  849.5 236.5 %all-reduce.2.cloned.1.call-done = f32[1024,1024]{0,1:T(8,128)} async-done(((f32[1024,1024]{0,1:T(8,128)}), f32[1024,1024]{0,1:T(8,128)}) %all-reduce.2.cloned.1.call-update) | async-done | bytes 4194320 | tf_op jit(solution)/shard_map/psum | solution.py:66
  1086.0 9.2 fusion.14
  1095.2 3.2 subtract_convert_fusion
  1098.3 0.0 all-gather.11.cloned.1.call-update
  1098.4 64.1 %all-gather.11.cloned.1.call-done = bf16[1024,1024]{1,0:T(8,128)(2,1)} async-done(((bf16[32,1024]{1,0:T(8,128)(2,1)}), bf16[1024,1024]{1,0:T(8,128)(2,1)}) %all-gather.11.cloned.1.call-update) | async-done | bytes 2097168 | tf_op jit(solution)/shard_map/all_gather | solution.py:77
  1162.4 3.1 copy.15
  (4 shorter events, 0.0 us)
Async XLA Ops:
  8.0 1087.2 %copy-start = (bf16[32,1024]{1,0:T(8,128)(2,1)S(1)}, bf16[32,1024]{1,0:T(8,128)(2,1)}, u32[]{:S(2)}) copy-start(bf16[32,1024]{1,0:T(8,128)(2,1)} %param.14) | copy-start | bytes 196612
  8.0 194.7 %all-gather.5.cloned.1.call-start = ((), (), s32[]{:S(2)}) async-start(), calls=%async_computation.2 | async-start | bytes 18874368 | tf_op jit(solution)/shard_map/all_gather | solution.py:37
  8.7 405.2 %reduce-scatter.3.cloned.1.call-start = ((), (), s32[]{:S(2)}) async-start(), calls=%async_computation.3 | async-start | bytes 18874368 | tf_op jit(solution)/shard_map/reduce_scatter | solution.py:41
  220.3 390.6 %all-gather.7.cloned.1.call-start = ((), (), s32[]{:S(2)}) async-start(), calls=%async_computation.4 | async-start | bytes 18874368 | tf_op jit(solution)/shard_map/all_gather | solution.py:37
  420.7 417.9 %reduce-scatter.5.cloned.1.call-start = ((), (), s32[]{:S(2)}) async-start(), calls=%async_computation.5 | async-start | bytes 18874368 | tf_op jit(solution)/shard_map/reduce_scatter | solution.py:41
  641.7 207.7 %all-gather.9.cloned.1.call-start = ((), (), s32[]{:S(2)}) async-start(), calls=%async_computation.7 | async-start | bytes 2162688 | tf_op jit(solution)/shard_map/all_gather | solution.py:65
  642.3 443.7 %all-reduce.2.cloned.1.call-start = ((), (), s32[]{:S(2)}) async-start(), calls=%async_computation.6 | async-start | bytes 8388608 | tf_op jit(solution)/shard_map/psum | solution.py:66
  849.2 313.3 %all-gather.11.cloned.1.call-start = ((), (), s32[]{:S(2)}) async-start(), calls=%async_computation.8 | async-start | bytes 2162688 | tf_op jit(solution)/shard_map/all_gather | solution.py:77
  849.4 245.7 %copy-start.1 = (f32[32,1024]{1,0:T(8,128)S(1)}, f32[32,1024]{1,0:T(8,128)}, u32[]{:S(2)}) copy-start(f32[32,1024]{1,0:T(8,128)} %param.13) | copy-start | bytes 393220
Sparse Core Ops, SparseCore 0:
  11.5 191.1 all-gather.4
  220.4 193.4 reduce-scatter.2
  420.8 189.9 all-gather.6
  641.9 196.6 reduce-scatter.4
Sparse Core Ops, SparseCore 1:
  644.1 78.4 all-gather.8
  849.3 236.7 all-reduce.1
  1098.5 63.9 all-gather.10
where the time goes:
time: 1170 us
  waiting for transfers between devices  1060 us (91%)
  matrix products  60.7 us (5%)
  other arithmetic  17.3 us (1%)
  between operations  15.5 us (1%)
  local copies, waits for them, and re-layouts  14.6 us (1%)
    all_gather x2, waiting for transfers between devices, shards(): lax.all_gather(rounded, 'fsdp', axis=0, tiled=True)  383 us
    reduce_scatter x2, waiting for transfers between devices, shards(): lax.psum_scatter(lax.dot_general(features, residual_grad, (((0,), (0,)),...  379 us
    psum x1, waiting for transfers between devices, shards(): total = lax.psum(change, 'rep')  236 us
    all_gather x1, waiting for transfers between devices, shards(): new_params = lax.all_gather(own_new, 'rep', axis=0, tiled=True)  64.1 us
    dot_general x2, matrix products, shards(): lax.dot_general(features, residual_grad, (((0,), (0,)), ((), ())), prefer...  48.4 us
  transfers between devices with their start and end apart: 7, of which 6 were waited for; matrix products, arithmetic and copies ran while one was open for 2% of the time, Pallas kernels for 0%

commit v1 on v0

v1 whole, which is shorter than its diff:
```python
import jax
import jax.numpy as jnp
from jax import lax
from jax.sharding import PartitionSpec as P

INNER = 2
CHUNKS = 2

inner_rate = 0.01
beta_one = 0.9
beta_two = 0.95
adam_eps = 1e-08
decay_rate = 0.1
outer_rate = 0.7
outer_mom = 0.9


def exchange(pieces, axis, groups=None):
    return lax.all_to_all(pieces, axis, 0, 0, tiled=True, axis_index_groups=groups)


def spread(piece, axis, count, groups=None):
    return exchange(jnp.broadcast_to(piece[None], (count,) + piece.shape), axis, groups)


def shards(
    global_params, first_moment, second_moment, batch, labels, momentum, left_root, right_root
):
    rows, width = global_params.shape
    tokens = batch.shape[2]
    fsdp = lax.axis_size("fsdp")
    replicas = lax.axis_size("rep")
    owned = rows // replicas
    total_tokens = tokens * fsdp
    cols = width // CHUNKS
    own_index = lax.axis_index("rep")
    core = own_index % 2
    swap = [(i, i ^ 1) for i in range(replicas)]
    chips = replicas // 2
    same_core = [[2 * k + c for k in range(chips)] for c in range(2)]

    features = []
    for step in range(INNER):
        split = batch[0, step].reshape(tokens, fsdp, rows).transpose(1, 0, 2)
        features.append(exchange(split, "fsdp").reshape(total_tokens, rows))

    outer = jnp.stack([left_root, right_root[0], momentum.astype(jnp.bfloat16)])
    outer_full = lax.all_gather(outer, "rep", axis=1, tiled=True)
    left_full, right_full, momentum_full = outer_full[0], outer_full[1], outer_full[2]

    start_weights = global_params.astype(jnp.float32)
    state = []
    for chunk in range(CHUNKS):
        part = slice(chunk * cols, (chunk + 1) * cols)
        state.append(
            (
                start_weights[:, part],
                first_moment[0][:, part].astype(jnp.float32),
                second_moment[0][:, part].astype(jnp.float32),
            )
        )
    for step in range(INNER):
        count = step + 1
        for chunk in range(CHUNKS):
            weights, moment_one, moment_two = state[chunk]
            partial = jnp.dot(
                features[step], weights.astype(jnp.bfloat16), preferred_element_type=jnp.float32
            ).astype(jnp.bfloat16)
            arrived = exchange(partial.reshape(fsdp, tokens, cols), "fsdp")
            projected = jnp.sum(arrived.astype(jnp.float32), axis=0)
            columns = jnp.arange(cols, dtype=jnp.int32) + chunk * cols
            target = (labels[0, step][:, None] == columns[None, :]).astype(jnp.float32)
            residual = ((projected - target) / total_tokens).astype(jnp.bfloat16)
            residual = spread(residual, "fsdp", fsdp).reshape(total_tokens, cols)
            grad = lax.dot_general(
                features[step], residual, (((0,), (0,)), ((), ())), preferred_element_type=jnp.float32
            )
            moment_one = beta_one * moment_one + (1.0 - beta_one) * grad
            moment_two = beta_two * moment_two + (1.0 - beta_two) * grad * grad
            corrected_one = moment_one / (1.0 - beta_one**count)
            corrected_two = moment_two / (1.0 - beta_two**count)
            weights = weights - inner_rate * (
                corrected_one / (jnp.sqrt(corrected_two) + adam_eps) + decay_rate * weights
            )
            state[chunk] = (weights, moment_one, moment_two)
    precond = jnp.zeros((rows, width), jnp.float32)
    half = rows // 2
    for chunk in range(CHUNKS):
        part = slice(chunk * cols, (chunk + 1) * cols)
        change = (start_weights[:, part] - state[chunk][0]).reshape(2, half, cols)
        other = lax.dynamic_index_in_dim(change, 1 - core, 0, keepdims=False).astype(jnp.bfloat16)
        mine = lax.dynamic_index_in_dim(change, core, 0, keepdims=False)
        pair = (mine + lax.ppermute(other, "rep", swap).astype(jnp.float32)).astype(jnp.bfloat16)
        arrived = exchange(pair.reshape(chips, half // chips, cols), "rep", same_core)
        total = jnp.sum(arrived.astype(jnp.float32), axis=0)
        averaged = (total / replicas).astype(jnp.bfloat16)
        mine = spread(averaged, "rep", chips, same_core).reshape(half, cols)
        other = lax.ppermute(mine, "rep", swap)
        full = jnp.concatenate(
            [jnp.where(core == 0, mine, other), jnp.where(core == 0, other, mine)], axis=0
        )
        left_part = jnp.dot(left_full, full, preferred_element_type=jnp.float32)
        high = left_part.astype(jnp.bfloat16)
        low = (left_part - high.astype(jnp.float32)).astype(jnp.bfloat16)
        right_rows = right_full[part]
        precond = (
            precond
            + jnp.dot(high, right_rows, preferred_element_type=jnp.float32)
            + jnp.dot(low, right_rows, preferred_element_type=jnp.float32)
        )
    new_params = (
        start_weights
        - outer_rate
        * (
            precond
            + outer_mom * (outer_mom * momentum_full.astype(jnp.float32) + precond)
        )
    ).astype(jnp.bfloat16)
    own = lax.dynamic_slice_in_dim(precond, own_index * owned, owned, 0)
    new_momentum = outer_mom * momentum + own
    return (new_params, new_momentum)


def solution(mesh):
    in_specs = (
        P("fsdp", None),
        P("rep", "fsdp", None),
        P("rep", "fsdp", None),
        P("rep", None, "fsdp", None),
        P("rep", None, "fsdp"),
        P(("fsdp", "rep"), None),
        P(("fsdp", "rep"), None),
        P("fsdp", "rep", None),
    )
    out_specs = (P("fsdp", None), P(("fsdp", "rep"), None))
    return jax.shard_map(shards, mesh=mesh, in_specs=in_specs, out_specs=out_specs, check_vma=False)
```

time: 1170 us -> 446 us (0.38)
  waiting for transfers between devices: 1060 us -> 167 us
  starting transfers between devices: 0.69 us -> 97.2 us
  local copies, waits for them, and re-layouts: 14.6 us -> 83.9 us
    all_gather x4 -> x1, waiting for transfers between devices: 447 us -> 0.01 us  [shards(): outer_full = lax.all_gather(outer, 'rep', axis=1, tiled=True)]
    reduce_scatter x2 -> x0, waiting for transfers between devices: 379 us -> none  [shards(): lax.psum_scatter(lax.dot_general(features, residual_grad, (((0,), (0,)),...]
    psum x1 -> x0, waiting for transfers between devices: 236 us -> none  [shards(): total = lax.psum(change, 'rep')]
    all_to_all x0 -> x14, waiting for transfers between devices: none -> 167 us  [exchange(): lax.all_to_all(pieces, axis, 0, 0, tiled=True, axis_index_groups=groups)]
    all_to_all x0 -> x14, starting transfers between devices: none -> 89.3 us  [exchange(): lax.all_to_all(pieces, axis, 0, 0, tiled=True, axis_index_groups=groups)]
    unnamed x8 -> x45, local copies, waits for them, and re-layouts: 13.9 us -> 35.2 us
    dynamic_slice x0 -> x5, local copies, waits for them, and re-layouts: none -> 17.1 us  [the longest x4 12 us: shards(): mine = lax.dynamic_index_in_dim(change, core, 0, keepdims=False)]
    dot_general x4 -> x14, matrix products: 60.7 us -> 57 us  [the longest x4 24.2 us: shards(): lax.dot_general(features[step], residual, (((0,), (0,)), ((), ())), prefe...]
  transfers between devices with their start and end apart: 7 -> 19, of which waited for: 6 -> 14; matrix products, arithmetic and copies ran while one was open for 2% -> 26% of each run, Pallas kernels for 0% -> 0%
where the time goes in v1:
time: 446 us; the launch traced here: 439 us
  waiting for transfers between devices  167 us (37%)
  starting transfers between devices  97.2 us (22%)
  local copies, waits for them, and re-layouts  83.9 us (19%)
  matrix products  57 us (13%)
  other arithmetic  18.8 us (4%)
  between operations  14.7 us (3%)
    all_to_all x14, waiting for transfers between devices, exchange(): lax.all_to_all(pieces, axis, 0, 0, tiled=True, axis_index_groups=groups)  167 us
    all_to_all x14, starting transfers between devices, exchange(): lax.all_to_all(pieces, axis, 0, 0, tiled=True, axis_index_groups=groups)  89.3 us
    unnamed x45, local copies, waits for them, and re-layouts  35.2 us
    dot_general x4, matrix products, shards(): lax.dot_general(features[step], residual, (((0,), (0,)), ((), ())), prefe...  24.2 us
    dot_general x4, matrix products, shards(): jnp.dot(features[step], weights.astype(jnp.bfloat16), preferred_element_t...  18.9 us
    dynamic_slice x4, local copies, waits for them, and re-layouts, shards(): mine = lax.dynamic_index_in_dim(change, core, 0, keepdims=False)  12 us
  transfers between devices with their start and end apart: 19, of which 14 were waited for; matrix products, arithmetic and copies ran while one was open for 26% of the time, Pallas kernels for 0%

profile of v1, /device:TPU:1, one launch (start us, length us, event | category | flops | bytes accessed | tf_op | source)
XLA Modules:
  0.0 439.0 jit_solution(2171461403048667470)
XLA Ops:
  7.2 4.7 %fusion.48 = (bf16[1,1,128,8192]{3,2,1,0:T(8,128)(2,1)}, bf16[1,1,128,8192]{3,2,1,0:T(8,128)(2,1)}) fusion(bf16[1,2,128,8192]{3,2,1,0:T(8,128)(2,1)} %param.11), kind=kLoop, calls=%fused_computation.107 | loop fusion | bytes 8388608 | tf_op jit(solution)/shard_map/slice | solution.py:44
  17.7 7.5 %all-to-all-start = ((bf16[8,128,1024]{2,1,0:T(8,128)(2,1)}), bf16[8,128,1024]{2,1,0:T(8,128)(2,1)}, u32[]{:S(2)}, u32[]{:S(2)}) async-start(bf16[8,128,1024]{2,1,0:T(8,128)(2,1)} %bitcast.5), calls=%async_computation | async-start | bytes 4194304 | tf_op jit(solution)/shard_map/all_to_all | solution.py:19
  30.6 20.8 %all-to-all-done = bf16[8,128,1024]{2,1,0:T(8,128)(2,1)} async-done(((bf16[8,128,1024]{2,1,0:T(8,128)(2,1)}), bf16[8,128,1024]{2,1,0:T(8,128)(2,1)}, u32[]{:S(2)}, u32[]{:S(2)}) %all-to-all-start) | async-done | bytes 2097184 | tf_op jit(solution)/shard_map/all_to_all | solution.py:19
  55.9 5.2 %all-to-all-start.8 = ((bf16[8,128,512]{2,1,0:T(8,128)(2,1)}), bf16[8,128,512]{2,1,0:T(8,128)(2,1)S(1)}, u32[]{:S(2)}, u32[]{:S(2)}) async-start(bf16[8,128,512]{2,1,0:T(8,128)(2,1)} %bitcast.178), calls=%async_computation.8 | async-start | bytes 2097152 | tf_op jit(solution)/shard_map/all_to_all | solution.py:19
  61.1 4.5 %convolution_convert_fusion.3 = bf16[1024,512]{1,0:T(8,128)(2,1)} fusion(bf16[1024,1024]{1,0:T(8,128)(2,1)} %bitcast.6, f32[1024,1024]{0,1:T(8,128)} %convert_element_type.185), kind=kOutput, calls=%fused_computation.53 | convolution fusion | flops 1074266112 | bytes 4194304 | tf_op jit(solution)/shard_map/dot_general | solution.py:66
  65.6 9.9 %all-to-all-done.8 = bf16[8,128,512]{2,1,0:T(8,128)(2,1)S(1)} async-done(((bf16[8,128,512]{2,1,0:T(8,128)(2,1)}), bf16[8,128,512]{2,1,0:T(8,128)(2,1)S(1)}, u32[]{:S(2)}, u32[]{:S(2)}) %all-to-all-start.8) | async-done | bytes 1048608 | tf_op jit(solution)/shard_map/all_to_all | solution.py:19
  75.5 5.7 %all-to-all-start.1 = ((bf16[8,128,512]{2,1,0:T(8,128)(2,1)}), bf16[8,128,512]{2,1,0:T(8,128)(2,1)}, u32[]{:S(2)}, u32[]{:S(2)}) async-start(bf16[8,128,512]{2,1,0:T(8,128)(2,1)} %bitcast.177), calls=%async_computation.1 | async-start | bytes 2097152 | tf_op jit(solution)/shard_map/all_to_all | solution.py:19
  89.2 6.5 %all-to-all-done.1 = bf16[8,128,512]{2,1,0:T(8,128)(2,1)} async-done(((bf16[8,128,512]{2,1,0:T(8,128)(2,1)}), bf16[8,128,512]{2,1,0:T(8,128)(2,1)}, u32[]{:S(2)}, u32[]{:S(2)}) %all-to-all-start.1) | async-done | bytes 1048608 | tf_op jit(solution)/shard_map/all_to_all | solution.py:19
  95.7 5.9 %all-to-all-start.3 = ((bf16[8,128,1024]{2,1,0:T(8,128)(2,1)}), bf16[8,128,1024]{2,1,0:T(8,128)(2,1)}, u32[]{:S(2)}, u32[]{:S(2)}) async-start(bf16[8,128,1024]{2,1,0:T(8,128)(2,1)} %bitcast.159), calls=%async_computation.3 | async-start | bytes 4194304 | tf_op jit(solution)/shard_map/all_to_all | solution.py:19
  103.5 24.4 %all-to-all-done.3 = bf16[8,128,1024]{2,1,0:T(8,128)(2,1)} async-done(((bf16[8,128,1024]{2,1,0:T(8,128)(2,1)}), bf16[8,128,1024]{2,1,0:T(8,128)(2,1)}, u32[]{:S(2)}, u32[]{:S(2)}) %all-to-all-start.3) | async-done | bytes 2097184 | tf_op jit(solution)/shard_map/all_to_all | solution.py:19
  129.0 5.2 %all-to-all-start.9 = ((bf16[8,128,512]{1,2,0:T(8,128)(2,1)}), bf16[8,128,512]{1,2,0:T(8,128)(2,1)S(1)}, u32[]{:S(2)}, u32[]{:S(2)}) async-start(bf16[8,128,512]{1,2,0:T(8,128)(2,1)} %broadcast_in_dim.15), calls=%async_computation.9 | async-start | bytes 2097152 | tf_op jit(solution)/shard_map/all_to_all | solution.py:19
  143.9 4.7 %all-to-all-done.9 = bf16[8,128,512]{1,2,0:T(8,128)(2,1)S(1)} async-done(((bf16[8,128,512]{1,2,0:T(8,128)(2,1)}), bf16[8,128,512]{1,2,0:T(8,128)(2,1)S(1)}, u32[]{:S(2)}, u32[]{:S(2)}) %all-to-all-start.9) | async-done | bytes 1048608 | tf_op jit(solution)/shard_map/all_to_all | solution.py:19
  149.7 5.7 %all-to-all-start.2 = ((bf16[8,128,512]{1,2,0:T(8,128)(2,1)}), bf16[8,128,512]{1,2,0:T(8,128)(2,1)}, u32[]{:S(2)}, u32[]{:S(2)}) async-start(bf16[8,128,512]{1,2,0:T(8,128)(2,1)} %broadcast_in_dim.12), calls=%async_computation.2 | async-start | bytes 2097152 | tf_op jit(solution)/shard_map/all_to_all | solution.py:19
  159.1 4.7 %fusion.28 = bf16[64,8,8,128]{3,2,1,0:T(8,128)(2,1)S(1)} fusion(bf16[1024,1024]{1,0:T(8,128)(2,1)} %bitcast.15, f32[1024,1024]{0,1:T(8,128)S(1)} %copy-done.1, f32[512,1024,1]{1,0,2:T(8,128)S(1)} %fusion.50, bf16[1024,1024]{0,1:T(8,128)(2,1)S(1)} %bitcast.170, bf16[1024,1024]{0,1:T(8,128)(2,1)} %bitcast.172), kind=kOutput, calls=%fused_computation.55 | convolution fusion | flops 1083703296 | bytes 9437184 | tf_op jit(solution)/shard_map/dot_general | solution.py:66
  165.0 16.8 %all-to-all-done.2 = bf16[8,128,512]{1,2,0:T(8,128)(2,1)} async-done(((bf16[8,128,512]{1,2,0:T(8,128)(2,1)}), bf16[8,128,512]{1,2,0:T(8,128)(2,1)}, u32[]{:S(2)}, u32[]{:S(2)}) %all-to-all-start.2) | async-done | bytes 1048608 | tf_op jit(solution)/shard_map/all_to_all | solution.py:19
  190.1 5.3 %fusion.27 = bf16[64,8,8,128]{3,2,1,0:T(8,128)(2,1)S(1)} fusion(bf16[1024,1024]{1,0:T(8,128)(2,1)} %bitcast.15, f32[1024,1024]{0,1:T(8,128)S(1)} %copy-done.2, f32[512,1024,1]{1,0,2:T(8,128)S(1)} %fusion.49, bf16[1024,1024]{0,1:T(8,128)(2,1)S(1)} %bitcast.171, bf16[1024,1024]{0,1:T(8,128)(2,1)} %bitcast.173), kind=kOutput, calls=%fused_computation.54 | convolution fusion | flops 1083703296 | bytes 9437184 | tf_op jit(solution)/shard_map/dot_general | solution.py:66
  196.6 14.7 %all-to-all-done.10 = bf16[8,128,512]{1,2,0:T(8,128)(2,1)S(1)} async-done(((bf16[8,128,512]{1,2,0:T(8,128)(2,1)}), bf16[8,128,512]{1,2,0:T(8,128)(2,1)S(1)}, u32[]{:S(2)}, u32[]{:S(2)}) %all-to-all-start.10) | async-done | bytes 1048608 | tf_op jit(solution)/shard_map/all_to_all | solution.py:19
  215.8 13.0 %all-to-all-done.4 = bf16[8,128,512]{1,2,0:T(8,128)(2,1)} async-done(((bf16[8,128,512]{1,2,0:T(8,128)(2,1)}), bf16[8,128,512]{1,2,0:T(8,128)(2,1)}, u32[]{:S(2)}, u32[]{:S(2)}) %all-to-all-start.4) | async-done | bytes 1048608 | tf_op jit(solution)/shard_map/all_to_all | solution.py:19
  231.8 6.8 %all-to-all-start.5 = ((bf16[8,128,512]{1,2,0:T(8,128)(2,1)}), bf16[8,128,512]{1,2,0:T(8,128)(2,1)S(1)}, u32[]{:S(2)}, u32[]{:S(2)}) async-start(bf16[8,128,512]{1,2,0:T(8,128)(2,1)} %broadcast_in_dim.13), calls=%async_computation.5 | async-start | bytes 2097152 | tf_op jit(solution)/shard_map/all_to_all | solution.py:19
  238.7 14.3 %all-to-all-done.5 = bf16[8,128,512]{1,2,0:T(8,128)(2,1)S(1)} async-done(((bf16[8,128,512]{1,2,0:T(8,128)(2,1)}), bf16[8,128,512]{1,2,0:T(8,128)(2,1)S(1)}, u32[]{:S(2)}, u32[]{:S(2)}) %all-to-all-start.5) | async-done | bytes 1048608 | tf_op jit(solution)/shard_map/all_to_all | solution.py:19
  254.1 5.7 %all-to-all-start.11 = ((bf16[8,128,512]{1,2,0:T(8,128)(2,1)}), bf16[8,128,512]{1,2,0:T(8,128)(2,1)}, u32[]{:S(2)}, u32[]{:S(2)}) async-start(bf16[8,128,512]{1,2,0:T(8,128)(2,1)} %broadcast_in_dim.16), calls=%async_computation.11 | async-start | bytes 2097152 | tf_op jit(solution)/shard_map/all_to_all | solution.py:19
  259.8 8.6 %subtract_subtract_fusion.1 = f32[1024,512]{0,1:T(8,128)} fusion(f32[1024,1024]{0,1:T(8,128)} %convert_element_type.185, bf16[8,128,512]{1,2,0:T(8,128)(2,1)S(1)} %all-to-all-done.5, bf16[8,128,1024]{2,1,0:T(8,128)(2,1)} %all-to-all-done.3, f32[512,1024,1]{1,0,2:T(8,128)} %copy-done.14, bf16[1024,1024]{0,1:T(8,128)(2,1)} %bitcast.168, ...), kind=kOutput, calls=%fused_computation.42 | convolution fusion | flops 1091043328 | bytes 11534336 | tf_op jit(solution)/shard_map/dot_general | solution.py:75
  274.3 9.3 %subtract_subtract_fusion = f32[1024,512]{0,1:T(8,128)} fusion(f32[1024,1024]{0,1:T(8,128)} %convert_element_type.185, bf16[8,128,512]{1,2,0:T(8,128)(2,1)} %all-to-all-done.11, bf16[8,128,1024]{2,1,0:T(8,128)(2,1)} %all-to-all-done.3, f32[512,1024,1]{1,0,2:T(8,128)} %copy-done.13, bf16[1024,1024]{0,1:T(8,128)(2,1)} %bitcast.169, ...), kind=kOutput, calls=%fused_computation.37 | convolution fusion | flops 1091043328 | bytes 11534336 | tf_op jit(solution)/shard_map/dot_general | solution.py:75
  287.5 5.1 %constant_dynamic-slice_fusion = (bf16[1,512,512]{1,0,2:T(2,128)(2,1)S(1)}, bf16[1,512,512]{1,0,2:T(2,128)(2,1)}) fusion(f32[2,512,512]{1,0,2:T(2,128)} %reshape.194, s32[]{:T(128)S(6)} %select_n.42, f32[2,512,512]{1,0,2:T(2,128)} %reshape.189), kind=kLoop, calls=%fused_computation.99 | loop fusion | bytes 2097156 | tf_op jit(solution)/shard_map/jit(dynamic_index_in_dim)/dynamic_slice | solution.py:91
  307.9 14.0 %all-to-all-start.6 = ((bf16[16,32,512]{2,1,0:T(8,128)(2,1)}), bf16[16,32,512]{2,1,0:T(8,128)(2,1)}, u32[]{:S(2)}, u32[]{:S(2)}) async-start(bf16[16,32,512]{2,1,0:T(8,128)(2,1)} %bitcast.176), calls=%async_computation.6 | async-start | bytes 1048576 | tf_op jit(solution)/shard_map/all_to_all | solution.py:19
  331.7 4.7 %all-to-all-done.6 = bf16[16,32,512]{2,1,0:T(8,128)(2,1)} async-done(((bf16[16,32,512]{2,1,0:T(8,128)(2,1)}), bf16[16,32,512]{2,1,0:T(8,128)(2,1)}, u32[]{:S(2)}, u32[]{:S(2)}) %all-to-all-start.6) | async-done | bytes 524320 | tf_op jit(solution)/shard_map/all_to_all | solution.py:19
  336.5 6.0 %all-to-all-start.12 = ((bf16[16,32,512]{2,1,0:T(8,128)(2,1)}), bf16[16,32,512]{2,1,0:T(8,128)(2,1)S(1)}, u32[]{:S(2)}, u32[]{:S(2)}) async-start(bf16[16,32,512]{2,1,0:T(8,128)(2,1)} %bitcast.36), calls=%async_computation.12 | async-start | bytes 1048576 | tf_op jit(solution)/shard_map/all_to_all | solution.py:19
  343.6 12.1 %all-to-all-done.12 = bf16[16,32,512]{2,1,0:T(8,128)(2,1)S(1)} async-done(((bf16[16,32,512]{2,1,0:T(8,128)(2,1)}), bf16[16,32,512]{2,1,0:T(8,128)(2,1)S(1)}, u32[]{:S(2)}, u32[]{:S(2)}) %all-to-all-start.12) | async-done | bytes 524320 | tf_op jit(solution)/shard_map/all_to_all | solution.py:19
  356.5 6.7 %all-to-all-start.7 = ((bf16[16,32,512]{2,1,0:T(8,128)(2,1)}), bf16[16,32,512]{2,1,0:T(8,128)(2,1)S(1)}, u32[]{:S(2)}, u32[]{:S(2)}) async-start(bf16[16,32,512]{2,1,0:T(8,128)(2,1)} %broadcast_in_dim.14), calls=%async_computation.7 | async-start | bytes 1048576 | tf_op jit(solution)/shard_map/all_to_all | solution.py:19
  363.3 12.7 %all-to-all-done.7 = bf16[16,32,512]{2,1,0:T(8,128)(2,1)S(1)} async-done(((bf16[16,32,512]{2,1,0:T(8,128)(2,1)}), bf16[16,32,512]{2,1,0:T(8,128)(2,1)S(1)}, u32[]{:S(2)}, u32[]{:S(2)}) %all-to-all-start.7) | async-done | bytes 524320 | tf_op jit(solution)/shard_map/all_to_all | solution.py:19
  376.8 6.3 %all-to-all-start.13 = ((bf16[16,32,512]{2,1,0:T(8,128)(2,1)}), bf16[16,32,512]{2,1,0:T(8,128)(2,1)S(1)}, u32[]{:S(2)}, u32[]{:S(2)}) async-start(bf16[16,32,512]{2,1,0:T(8,128)(2,1)} %broadcast_in_dim.17), calls=%async_computation.13 | async-start | bytes 1048576 | tf_op jit(solution)/shard_map/all_to_all | solution.py:19
  385.3 10.8 %all-to-all-done.13 = bf16[16,32,512]{2,1,0:T(8,128)(2,1)S(1)} async-done(((bf16[16,32,512]{2,1,0:T(8,128)(2,1)}), bf16[16,32,512]{2,1,0:T(8,128)(2,1)S(1)}, u32[]{:S(2)}, u32[]{:S(2)}) %all-to-all-start.13) | async-done | bytes 524320 | tf_op jit(solution)/shard_map/all_to_all | solution.py:19
  (112 shorter events, 135.9 us)
Async XLA Ops:
  17.7 33.7 %all-to-all-start = ((bf16[8,128,1024]{2,1,0:T(8,128)(2,1)}), bf16[8,128,1024]{2,1,0:T(8,128)(2,1)}, u32[]{:S(2)}, u32[]{:S(2)}) async-start(bf16[8,128,1024]{2,1,0:T(8,128)(2,1)} %bitcast.5), calls=%async_computation | async-start | bytes 4194304 | tf_op jit(solution)/shard_map/all_to_all | solution.py:19
  55.9 19.6 %all-to-all-start.8 = ((bf16[8,128,512]{2,1,0:T(8,128)(2,1)}), bf16[8,128,512]{2,1,0:T(8,128)(2,1)S(1)}, u32[]{:S(2)}, u32[]{:S(2)}) async-start(bf16[8,128,512]{2,1,0:T(8,128)(2,1)} %bitcast.178), calls=%async_computation.8 | async-start | bytes 2097152 | tf_op jit(solution)/shard_map/all_to_all | solution.py:19
  75.5 20.2 %all-to-all-start.1 = ((bf16[8,128,512]{2,1,0:T(8,128)(2,1)}), bf16[8,128,512]{2,1,0:T(8,128)(2,1)}, u32[]{:S(2)}, u32[]{:S(2)}) async-start(bf16[8,128,512]{2,1,0:T(8,128)(2,1)} %bitcast.177), calls=%async_computation.1 | async-start | bytes 2097152 | tf_op jit(solution)/shard_map/all_to_all | solution.py:19
  95.7 5.9 %copy-start.12 = (s32[1,2,128]{2,1,0:T(2,128)S(1)}, s32[1,2,128]{2,1,0:T(2,128)}, u32[]{:S(2)}) copy-start(s32[1,2,128]{2,1,0:T(2,128)} %param.12) | copy-start | bytes 3076
  95.7 32.1 %all-to-all-start.3 = ((bf16[8,128,1024]{2,1,0:T(8,128)(2,1)}), bf16[8,128,1024]{2,1,0:T(8,128)(2,1)}, u32[]{:S(2)}, u32[]{:S(2)}) async-start(bf16[8,128,1024]{2,1,0:T(8,128)(2,1)} %bitcast.159), calls=%async_computation.3 | async-start | bytes 4194304 | tf_op jit(solution)/shard_map/all_to_all | solution.py:19
  103.2 31.1 %copy-start.10 = (f32[32,1024]{1,0:T(8,128)S(1)}, f32[32,1024]{1,0:T(8,128)}, u32[]{:S(2)}) copy-start(f32[32,1024]{1,0:T(8,128)} %param.13) | copy-start | bytes 393220
  103.2 31.1 %copy-start.11 = (bf16[1,32,1024]{2,1,0:T(8,128)(2,1)S(1)}, bf16[1,32,1024]{2,1,0:T(8,128)(2,1)}, u32[]{:S(2)}) copy-start(bf16[1,32,1024]{2,1,0:T(8,128)(2,1)} %param.15) | copy-start | bytes 196612
  129.0 19.6 %all-to-all-start.9 = ((bf16[8,128,512]{1,2,0:T(8,128)(2,1)}), bf16[8,128,512]{1,2,0:T(8,128)(2,1)S(1)}, u32[]{:S(2)}, u32[]{:S(2)}) async-start(bf16[8,128,512]{1,2,0:T(8,128)(2,1)} %broadcast_in_dim.15), calls=%async_computation.9 | async-start | bytes 2097152 | tf_op jit(solution)/shard_map/all_to_all | solution.py:19
  134.2 270.2 %all-gather.2.cloned.1.call-start = ((), (), s32[]{:S(2)}) async-start(), calls=%async_computation.14 | async-start | bytes 6488064 | tf_op jit(solution)/shard_map/all_gather | solution.py:48
  149.7 32.1 %all-to-all-start.2 = ((bf16[8,128,512]{1,2,0:T(8,128)(2,1)}), bf16[8,128,512]{1,2,0:T(8,128)(2,1)}, u32[]{:S(2)}, u32[]{:S(2)}) async-start(bf16[8,128,512]{1,2,0:T(8,128)(2,1)} %broadcast_in_dim.12), calls=%async_computation.2 | async-start | bytes 2097152 | tf_op jit(solution)/shard_map/all_to_all | solution.py:19
  155.5 3.1 copy-start.1
  155.5 3.6 copy-start.4
  158.5 5.3 %copy-start.13 = (f32[512,1024,1]{1,0,2:T(8,128)}, f32[512,1024,1]{1,0,2:T(8,128)S(1)}, u32[]{:S(2)}) copy-start(f32[512,1024,1]{1,0,2:T(8,128)S(1)} %fusion.50) | copy-start | bytes 6291460
  181.8 29.5 %all-to-all-start.10 = ((bf16[8,128,512]{1,2,0:T(8,128)(2,1)}), bf16[8,128,512]{1,2,0:T(8,128)(2,1)S(1)}, u32[]{:S(2)}, u32[]{:S(2)}) async-start(bf16[8,128,512]{1,2,0:T(8,128)(2,1)} %bitcast.164), calls=%async_computation.10 | async-start | bytes 2097152 | tf_op jit(solution)/shard_map/all_to_all | solution.py:19
  186.1 3.4 copy-start.2
  186.1 3.9 copy-start.5
  190.1 5.3 %copy-start.14 = (f32[512,1024,1]{1,0,2:T(8,128)}, f32[512,1024,1]{1,0,2:T(8,128)S(1)}, u32[]{:S(2)}) copy-start(f32[512,1024,1]{1,0,2:T(8,128)S(1)} %fusion.49) | copy-start | bytes 6291460
  211.3 17.6 %all-to-all-start.4 = ((bf16[8,128,512]{1,2,0:T(8,128)(2,1)}), bf16[8,128,512]{1,2,0:T(8,128)(2,1)}, u32[]{:S(2)}, u32[]{:S(2)}) async-start(bf16[8,128,512]{1,2,0:T(8,128)(2,1)} %bitcast.165), calls=%async_computation.4 | async-start | bytes 2097152 | tf_op jit(solution)/shard_map/all_to_all | solution.py:19
  231.8 21.2 %all-to-all-start.5 = ((bf16[8,128,512]{1,2,0:T(8,128)(2,1)}), bf16[8,128,512]{1,2,0:T(8,128)(2,1)S(1)}, u32[]{:S(2)}, u32[]{:S(2)}) async-start(bf16[8,128,512]{1,2,0:T(8,128)(2,1)} %broadcast_in_dim.13), calls=%async_computation.5 | async-start | bytes 2097152 | tf_op jit(solution)/shard_map/all_to_all | solution.py:19
  254.1 20.2 %all-to-all-start.11 = ((bf16[8,128,512]{1,2,0:T(8,128)(2,1)}), bf16[8,128,512]{1,2,0:T(8,128)(2,1)}, u32[]{:S(2)}, u32[]{:S(2)}) async-start(bf16[8,128,512]{1,2,0:T(8,128)(2,1)} %broadcast_in_dim.16), calls=%async_computation.11 | async-start | bytes 2097152 | tf_op jit(solution)/shard_map/all_to_all | solution.py:19
  296.1 9.4 %collective-permute-start = (bf16[512,512]{1,0:T(8,128)(2,1)}, bf16[512,512]{1,0:T(8,128)(2,1)}, u32[]{:S(2)}, u32[]{:S(2)}) collective-permute-start(bf16[512,512]{1,0:T(8,128)(2,1)} %bitcast.179), channel_id=1, source_target_pairs={{0,8},{8,0},{16,24},{24,16},{32,40},{40,32},{48,56},{56,48},{64,72... | collective-permute-start | bytes 1572872 | tf_op jit(solution)/shard_map/ppermute | solution.py:93
  307.9 28.5 %all-to-all-start.6 = ((bf16[16,32,512]{2,1,0:T(8,128)(2,1)}), bf16[16,32,512]{2,1,0:T(8,128)(2,1)}, u32[]{:S(2)}, u32[]{:S(2)}) async-start(bf16[16,32,512]{2,1,0:T(8,128)(2,1)} %bitcast.176), calls=%async_computation.6 | async-start | bytes 1048576 | tf_op jit(solution)/shard_map/all_to_all | solution.py:19
  324.2 5.2 %collective-permute-start.2 = (bf16[512,512]{1,0:T(8,128)(2,1)}, bf16[512,512]{1,0:T(8,128)(2,1)}, u32[]{:S(2)}, u32[]{:S(2)}) collective-permute-start(bf16[512,512]{1,0:T(8,128)(2,1)} %bitcast.180), channel_id=1, source_target_pairs={{0,8},{8,0},{16,24},{24,16},{32,40},{40,32},{48,56},{56,48},{64,72... | collective-permute-start | bytes 1572872 | tf_op jit(solution)/shard_map/ppermute | solution.py:93
  336.5 19.2 %all-to-all-start.12 = ((bf16[16,32,512]{2,1,0:T(8,128)(2,1)}), bf16[16,32,512]{2,1,0:T(8,128)(2,1)S(1)}, u32[]{:S(2)}, u32[]{:S(2)}) async-start(bf16[16,32,512]{2,1,0:T(8,128)(2,1)} %bitcast.36), calls=%async_computation.12 | async-start | bytes 1048576 | tf_op jit(solution)/shard_map/all_to_all | solution.py:19
  356.5 19.5 %all-to-all-start.7 = ((bf16[16,32,512]{2,1,0:T(8,128)(2,1)}), bf16[16,32,512]{2,1,0:T(8,128)(2,1)S(1)}, u32[]{:S(2)}, u32[]{:S(2)}) async-start(bf16[16,32,512]{2,1,0:T(8,128)(2,1)} %broadcast_in_dim.14), calls=%async_computation.7 | async-start | bytes 1048576 | tf_op jit(solution)/shard_map/all_to_all | solution.py:19
  376.8 19.3 %all-to-all-start.13 = ((bf16[16,32,512]{2,1,0:T(8,128)(2,1)}), bf16[16,32,512]{2,1,0:T(8,128)(2,1)S(1)}, u32[]{:S(2)}, u32[]{:S(2)}) async-start(bf16[16,32,512]{2,1,0:T(8,128)(2,1)} %broadcast_in_dim.17), calls=%async_computation.13 | async-start | bytes 1048576 | tf_op jit(solution)/shard_map/all_to_all | solution.py:19
  383.2 17.1 %collective-permute-start.1 = (bf16[512,512]{1,0:T(8,128)(2,1)S(1)}, bf16[512,512]{1,0:T(8,128)(2,1)}, u32[]{:S(2)}, u32[]{:S(2)}) collective-permute-start(bf16[512,512]{1,0:T(8,128)(2,1)S(1)} %bitcast.166), channel_id=1, source_target_pairs={{0,8},{8,0},{16,24},{24,16},{32,40},{40,32},{48,56},{56,48},{64,72... | collective-permute-start | bytes 1572872 | tf_op jit(solution)/shard_map/ppermute | solution.py:98
  396.1 6.2 %collective-permute-start.3 = (bf16[512,512]{1,0:T(8,128)(2,1)S(1)}, bf16[512,512]{1,0:T(8,128)(2,1)}, u32[]{:S(2)}, u32[]{:S(2)}) collective-permute-start(bf16[512,512]{1,0:T(8,128)(2,1)S(1)} %bitcast.167), channel_id=1, source_target_pairs={{0,8},{8,0},{16,24},{24,16},{32,40},{40,32},{48,56},{56,48},{64,72... | collective-permute-start | bytes 1572872 | tf_op jit(solution)/shard_map/ppermute | solution.py:98
  407.5 4.1 copy-start.6
  407.5 4.1 copy-start.7
  411.6 5.7 %slice-start = ((s8[6291456]{0:T(1024)(128)(4,1)}), s8[4194304]{0:T(1024)(128)(4,1)S(1)}, s32[]{:S(2)}) async-start(s8[6291456]{0:T(1024)(128)(4,1)} %bitcast.162), calls=%async_computation.15 | async-start | bytes 8388608
  425.8 4.0 copy-start.3
  (4 other events, 7.0 us)
Sparse Core Ops, SparseCore 0:
  136.9 77.7 all-gather.1

commit v2 on v0

v2 whole, which is shorter than its diff:
```python
import functools

import jax
import jax.numpy as jnp
from jax import lax
from jax.experimental import pallas as pl
from jax.experimental.pallas import tpu as pltpu
from jax.sharding import PartitionSpec as P

INNER = 2
BLOCK = 256
SCOPED = 28 * 1024 * 1024

inner_rate = 0.01
beta_one = 0.9
beta_two = 0.95
adam_eps = 1e-08
decay_rate = 0.1
outer_rate = 0.7
outer_mom = 0.9

f32 = jnp.float32
bf16 = jnp.bfloat16
ANY = pl.BlockSpec(memory_space=pl.ANY)


def params():
    return pltpu.CompilerParams(vmem_limit_bytes=SCOPED)


def cost(flops, size):
    return pl.CostEstimate(flops=flops, bytes_accessed=size, transcendentals=0)


def exchange(pieces, axis, groups=None):
    return lax.all_to_all(pieces, axis, 0, 0, tiled=True, axis_index_groups=groups)


def split_kernel(x_ref, o_ref):
    width = o_ref.shape[2]
    for piece in range(o_ref.shape[0]):
        o_ref[piece] = x_ref[0, 0, :, piece * width : (piece + 1) * width]


def split_batch(batch, step, pieces):
    tokens, total = batch.shape[2:]
    width = total // pieces
    per = pieces // 2
    return pl.pallas_call(
        split_kernel,
        grid=(2,),
        in_specs=[pl.BlockSpec((1, 1, tokens, per * width), lambda i: (0, step, 0, i))],
        out_specs=pl.BlockSpec((per, tokens, width), lambda i: (i, 0, 0)),
        out_shape=jax.ShapeDtypeStruct((pieces, tokens, width), batch.dtype),
        compiler_params=params(),
        cost_estimate=cost(0, 4 * tokens * total),
    )(batch)


def hold_kernel(x_ref, *refs):
    pass


def hold(x, *after):
    return pl.pallas_call(
        hold_kernel,
        in_specs=[ANY] * (1 + len(after)),
        out_specs=ANY,
        out_shape=jax.ShapeDtypeStruct(x.shape, x.dtype),
        input_output_aliases={0: 0},
        compiler_params=params(),
    )(x, *after)


def pack_kernel(place_ref, *refs):
    for side in range(2):
        out = refs[7 + side]
        for what in range(3):
            out[what] = refs[3 * side + what][...].reshape(out.shape[1:]).astype(bf16)


def pack(place, left, right, momentum, after):
    owned, width = left.shape
    half = width // 2

    def specs(side):
        def column(p):
            return lax.rem(p[0] + side, 2)

        return [
            pl.BlockSpec((owned, half), lambda i, p: (0, column(p))),
            pl.BlockSpec((1, owned, half), lambda i, p: (0, 0, column(p))),
            pl.BlockSpec((owned, half), lambda i, p: (0, column(p))),
        ]

    return pl.pallas_call(
        pack_kernel,
        grid_spec=pltpu.PrefetchScalarGridSpec(
            num_scalar_prefetch=1,
            grid=(1,),
            in_specs=specs(0) + specs(1) + [ANY],
            out_specs=[pl.BlockSpec((3, owned, half), lambda i, p: (0, 0, 0))] * 2,
        ),
        out_shape=[jax.ShapeDtypeStruct((3, owned, half), bf16)] * 2,
        compiler_params=params(),
        cost_estimate=cost(0, 16 * owned * width),
    )(place, *([left, right, momentum] * 2), after)


def flat(ref):
    return ref[...].reshape(-1, ref.shape[-1])


def partial_kernel(x_ref, w_ref, after_ref, o_ref):
    term = jnp.dot(flat(x_ref), w_ref[...], preferred_element_type=f32)
    o_ref[...] = term.astype(bf16).reshape(o_ref.shape)


def partial_of(features, weights, after):
    pieces, tokens, rows = features.shape
    width = weights.shape[1]
    per = pieces // 2
    return pl.pallas_call(
        partial_kernel,
        grid=(2,),
        in_specs=[
            pl.BlockSpec((per, tokens, rows), lambda i: (i, 0, 0)),
            pl.BlockSpec((rows, width), lambda i: (0, 0)),
            ANY,
        ],
        out_specs=pl.BlockSpec((per, tokens, width), lambda i: (i, 0, 0)),
        out_shape=jax.ShapeDtypeStruct((pieces, tokens, width), bf16),
        compiler_params=params(),
        cost_estimate=cost(2 * pieces * tokens * rows * width, 6 * rows * width),
    )(features, weights, after)


def residual_kernel(total_tokens, a_ref, l_ref, o_ref):
    count, tokens, cols = a_ref.shape
    projected = a_ref[0].astype(f32)
    for piece in range(1, count):
        projected = projected + a_ref[piece].astype(f32)
    columns = lax.broadcasted_iota(jnp.int32, (tokens, cols), 1) + pl.program_id(0) * cols
    target = jnp.where(l_ref[...] == columns, 1.0, 0.0)
    residual = ((projected - target) / total_tokens).astype(bf16)
    for piece in range(count):
        o_ref[piece] = residual


def spread_residual(arrived, labels, total_tokens):
    count, tokens, width = arrived.shape
    spec = pl.BlockSpec((count, tokens, width // 2), lambda i: (0, 0, i))
    return pl.pallas_call(
        functools.partial(residual_kernel, total_tokens),
        grid=(2,),
        in_specs=[spec, pl.BlockSpec((tokens, 1), lambda i: (0, 0))],
        out_specs=spec,
        out_shape=jax.ShapeDtypeStruct(arrived.shape, bf16),
        compiler_params=params(),
        cost_estimate=cost(0, 4 * arrived.size),
    )(arrived, labels)


def average_kernel(scale, a_ref, o_ref):
    total = a_ref[0].astype(f32)
    for piece in range(1, a_ref.shape[0]):
        total = total + a_ref[piece].astype(f32)
    averaged = (total / scale).astype(bf16)
    for piece in range(a_ref.shape[0]):
        o_ref[piece] = averaged


def spread_average(arrived, scale):
    return pl.pallas_call(
        functools.partial(average_kernel, scale),
        out_shape=jax.ShapeDtypeStruct(arrived.shape, bf16),
        compiler_params=params(),
        cost_estimate=cost(0, 4 * arrived.size),
    )(arrived)


def adam(count, grad, weights, moment_one, moment_two):
    moment_one = beta_one * moment_one + (1.0 - beta_one) * grad
    moment_two = beta_two * moment_two + ((1.0 - beta_two) * grad) * grad
    corrected = moment_two * (1.0 / (1.0 - beta_two**count))
    root = corrected * lax.rsqrt(corrected)
    scaled = (inner_rate / (1.0 - beta_one**count)) * moment_one
    weights = (1.0 - inner_rate * decay_rate) * weights - scaled * pltpu.reciprocal(root + adam_eps)
    return weights, moment_one, moment_two


def turned_dot(x, r):
    return lax.dot_general(x, r, (((0,), (0,)), ((), ())), preferred_element_type=f32)


def middle_kernel(x_ref, r_ref, w_ref, m_ref, v_ref, wo_ref, mo_ref, vo_ref, rounded_ref):
    weights, moment_one, moment_two = adam(
        1,
        turned_dot(flat(x_ref), flat(r_ref)),
        w_ref[...].astype(f32),
        m_ref[0].astype(f32),
        v_ref[0].astype(f32),
    )
    wo_ref[...] = weights
    mo_ref[...] = moment_one
    vo_ref[...] = moment_two
    rounded_ref[...] = weights.astype(bf16)


def middle(features, residual, weights, first, second):
    pieces, tokens, rows = features.shape
    width = weights.shape[1]
    block = BLOCK
    state = jax.ShapeDtypeStruct((rows, width), f32)
    state_spec = pl.BlockSpec((block, width), lambda i: (i, 0))
    moment_spec = pl.BlockSpec((1, block, width), lambda i: (0, i, 0))
    return pl.pallas_call(
        middle_kernel,
        grid=(rows // block,),
        in_specs=[
            pl.BlockSpec((pieces, tokens, block), lambda i: (0, 0, i)),
            pl.BlockSpec((pieces, tokens, width), lambda i: (0, 0, 0)),
            state_spec,
            moment_spec,
            moment_spec,
        ],
        out_specs=[state_spec] * 4,
        out_shape=[state] * 3 + [jax.ShapeDtypeStruct((rows, width), bf16)],
        compiler_params=params(),
        cost_estimate=cost(2 * pieces * tokens * rows * width, 26 * rows * width),
    )(features, residual, weights, first, second)


def last_kernel(place_ref, x_ref, r_ref, g_ref, w_ref, m_ref, v_ref, mine_ref, other_ref):
    grad = turned_dot(flat(x_ref), flat(r_ref))
    weights, _, _ = adam(INNER, grad, w_ref[...], m_ref[...], v_ref[...])
    change = g_ref[...].astype(f32) - weights
    step, half = pl.program_id(0), pl.num_programs(0) // 2

    @pl.when(step < half)
    def _():
        other_ref[...] = change.astype(bf16)

    @pl.when(step >= half)
    def _():
        mine_ref[...] = change


def last(place, features, residual, start, state):
    pieces, tokens, rows = features.shape
    width = start.shape[1]
    block = BLOCK
    steps = rows // block
    half = steps // 2

    def row(i, p):
        return lax.rem(i + half * (1 + p[0]), steps)

    state_spec = pl.BlockSpec((block, width), lambda i, p: (row(i, p), 0))
    return pl.pallas_call(
        last_kernel,
        grid_spec=pltpu.PrefetchScalarGridSpec(
            num_scalar_prefetch=1,
            grid=(steps,),
            in_specs=[
                pl.BlockSpec((pieces, tokens, block), lambda i, p: (0, 0, row(i, p))),
                pl.BlockSpec((pieces, tokens, width), lambda i, p: (0, 0, 0)),
            ]
            + [state_spec] * 4,
            out_specs=[
                pl.BlockSpec((block, width), lambda i, p: (jnp.maximum(i - half, 0), 0)),
                pl.BlockSpec((block, width), lambda i, p: (jnp.minimum(i, half - 1), 0)),
            ],
        ),
        out_shape=[
            jax.ShapeDtypeStruct((rows // 2, width), f32),
            jax.ShapeDtypeStruct((rows // 2, width), bf16),
        ],
        compiler_params=params(),
        cost_estimate=cost(2 * pieces * tokens * rows * width, 20 * rows * width),
    )(place, features, residual, start, *state)


def outer_kernel(
    place_ref, near_left, far_left, near_low, near_high, far_low, far_high, near_mom, far_mom,
    mine_ref, other_ref, g_ref, own_ref, new_ref, new_mom_ref, left, kept,
):
    side, row = pl.program_id(0), pl.program_id(1)
    half, width = mine_ref.shape

    def square(ref):
        return ref[...].reshape(half, half)

    @pl.when(side == 0)
    def _():
        left_part = jnp.dot(square(near_left), mine_ref[...], preferred_element_type=f32) + jnp.dot(
            square(far_left), other_ref[...], preferred_element_type=f32
        )
        left[row] = left_part.astype(bf16)

    def finish(first, second, mom_ref):
        precond = jnp.dot(left[row, :, :half], square(first), preferred_element_type=f32) + jnp.dot(
            left[row, :, half:], square(second), preferred_element_type=f32
        )
        momentum = outer_mom * square(mom_ref).astype(f32) + precond
        new_ref[...] = (
            g_ref[...].astype(f32) - outer_rate * (precond + outer_mom * momentum)
        ).astype(bf16)
        owned = own_ref.shape[0]
        per = half // owned

        @pl.when(row == place_ref[1] // per)
        def _():
            kept[...] = precond
            start = pl.multiple_of(lax.rem(place_ref[1], per) * owned, owned)
            new_mom_ref[...] = outer_mom * own_ref[...] + kept[pl.ds(start, owned), :]

    @pl.when(side == 0)
    def _():
        finish(near_low, near_high, near_mom)

    @pl.when(side == 1)
    def _():
        finish(far_low, far_high, far_mom)


def outer(place, near, far, mine, other, start, momentum):
    depth, _, cores, _, owned, half = near.shape
    width = mine.shape[1]

    def piece(what, row):
        return pl.BlockSpec(
            (depth, 1, cores, 1, owned, half), lambda j, i, p: (0, row(i), 0, what, 0, 0)
        )

    def here(i):
        return i

    def column(j, p):
        return lax.rem(p[0] + j, 2)

    low, high = (lambda i: 0), (lambda i: 1)
    whole = pl.BlockSpec((half, width), lambda j, i, p: (0, 0))
    own_spec = pl.BlockSpec((owned, half), lambda j, i, p: (0, column(j, p)))
    new_spec = pl.BlockSpec((half, half), lambda j, i, p: (i, column(j, p)))
    return pl.pallas_call(
        outer_kernel,
        grid_spec=pltpu.PrefetchScalarGridSpec(
            num_scalar_prefetch=1,
            grid=(2, 2),
            in_specs=[
                piece(0, here),
                piece(0, here),
                piece(1, low),
                piece(1, high),
                piece(1, low),
                piece(1, high),
                piece(2, here),
                piece(2, here),
                whole,
                whole,
                new_spec,
                own_spec,
            ],
            out_specs=[new_spec, own_spec],
            scratch_shapes=[
                pltpu.VMEM((2, half, width), bf16),
                pltpu.VMEM((half, half), f32),
            ],
        ),
        out_shape=[
            jax.ShapeDtypeStruct((2 * half, width), bf16),
            jax.ShapeDtypeStruct((owned, width), f32),
        ],
        compiler_params=params(),
        cost_estimate=cost(4 * width**3, 14 * width * width),
    )(place, near, far, near, near, far, far, near, far, mine, other, start, momentum)


def shards(
    global_params, first_moment, second_moment, batch, labels, momentum, left_root, right_root
):
    rows, width = global_params.shape
    tokens = batch.shape[2]
    fsdp = lax.axis_size("fsdp")
    replicas = lax.axis_size("rep")
    owned = rows // replicas
    total_tokens = tokens * fsdp
    half = rows // 2
    own_index = lax.axis_index("rep")
    core = own_index % 2
    upper = own_index // (replicas // 2)

    def stamp(kind):
        return jnp.stack([core, own_index, own_index * 4 + kind]).astype(jnp.int32)

    chips = replicas // 2
    depth = chips // 2
    swap = [(i, i ^ 1) for i in range(replicas)]
    beside = [(i, i ^ chips) for i in range(replicas)]
    same_core = [[2 * k + c for k in range(chips)] for c in range(2)]
    column = [[x * chips + 2 * z + c for z in range(depth)] for x in range(2) for c in range(2)]
    targets = [labels[0, step].reshape(tokens, 1) for step in range(INNER)]

    features = exchange(split_batch(batch, 0, fsdp), "fsdp")
    split = split_batch(batch, 1, fsdp)
    partial = partial_of(features, global_params, split)

    def ordered(index, own, partner):
        return jnp.where(index == 0, jnp.stack([own, partner]), jnp.stack([partner, own]))

    def own_residual(partial, step):
        return spread_residual(exchange(partial, "fsdp"), targets[step], total_tokens)

    own = own_residual(partial, 0)
    residual = exchange(own, "fsdp")
    kept, sent = pack(stamp(1), left_root, right_root, momentum, own)
    two = ordered(core, kept, lax.ppermute(sent, "rep", swap))
    four = ordered(upper, two, lax.ppermute(two, "rep", beside))
    near = lax.all_gather(four, "rep", axis=0, axis_index_groups=column)
    far = lax.ppermute(near, "rep", swap)
    following = exchange(hold(split, residual, four), "fsdp")
    *state, rounded = middle(features, residual, global_params, first_moment, second_moment)
    partial = partial_of(following, rounded, rounded)
    mine, sent = last(stamp(3), following, exchange(own_residual(partial, 1), "fsdp"), global_params, state)
    pair = (mine + lax.ppermute(sent, "rep", swap).astype(f32)).astype(bf16)
    arrived = exchange(pair.reshape(chips, owned, width), "rep", same_core)
    averaged = exchange(spread_average(arrived, replicas), "rep", same_core).reshape(half, width)
    other = lax.ppermute(averaged, "rep", swap)
    return tuple(outer(stamp(5), near, far, averaged, other, global_params, momentum))


def solution(mesh):
    in_specs = (
        P("fsdp", None),
        P("rep", "fsdp", None),
        P("rep", "fsdp", None),
        P("rep", None, "fsdp", None),
        P("rep", None, "fsdp"),
        P(("fsdp", "rep"), None),
        P(("fsdp", "rep"), None),
        P("fsdp", "rep", None),
    )
    out_specs = (P("fsdp", None), P(("fsdp", "rep"), None))
    return jax.shard_map(shards, mesh=mesh, in_specs=in_specs, out_specs=out_specs, check_vma=False)
```

time: 1170 us -> 334 us (0.29)
  waiting for transfers between devices: 1060 us -> 163 us
  matrix products: 60.7 us -> 0 us
  starting transfers between devices: 0.69 us -> 50.3 us
  Pallas kernels: 0 us -> 41.2 us
  blocking collectives: 0 us -> 30.5 us
  local copies, waits for them, and re-layouts: 14.6 us -> 31.7 us
  other arithmetic: 17.3 us -> 2.45 us
    all_gather x4 -> x1, waiting for transfers between devices: 447 us -> 0.02 us  [shards(): near = lax.all_gather(four, 'rep', axis=0, axis_index_groups=column)]
    reduce_scatter x2 -> x0, waiting for transfers between devices: 379 us -> none  [shards(): lax.psum_scatter(lax.dot_general(features, residual_grad, (((0,), (0,)),...]
    psum x1 -> x0, waiting for transfers between devices: 236 us -> none  [shards(): total = lax.psum(change, 'rep')]
    all_to_all x0 -> x7, waiting for transfers between devices: none -> 134 us  [exchange(): lax.all_to_all(pieces, axis, 0, 0, tiled=True, axis_index_groups=groups)]
    dot_general x4 -> x0, matrix products: 60.7 us -> none  [the longest x2 48.4 us: shards(): lax.dot_general(features, residual_grad, (((0,), (0,)), ((), ())), prefer...]
    all_to_all x0 -> x7, starting transfers between devices: none -> 43.8 us  [exchange(): lax.all_to_all(pieces, axis, 0, 0, tiled=True, axis_index_groups=groups)]
    pallas_call x0 -> x12, Pallas kernels: none -> 41.2 us  [the longest x1 10.1 us: outer(): pl.pallas_call(outer_kernel, grid_spec=pltpu.PrefetchScalarGridSpec(num_s...]
    all_to_all x0 -> x1, blocking collectives: none -> 30.5 us  [exchange(): lax.all_to_all(pieces, axis, 0, 0, tiled=True, axis_index_groups=groups)]
  transfers between devices with their start and end apart: 7 -> 13, of which waited for: 6 -> 10; matrix products, arithmetic and copies ran while one was open for 2% -> 1% of each run, Pallas kernels for 0% -> 6%
where the time goes in v2:
time: 334 us; the launch traced here: 333 us
  waiting for transfers between devices  163 us (49%)
  starting transfers between devices  50.3 us (15%)
  Pallas kernels  41.2 us (12%)
  local copies, waits for them, and re-layouts  31.7 us (9%)
  blocking collectives  30.5 us (9%)
  between operations  14.3 us (4%)
    all_to_all x7, waiting for transfers between devices, exchange(): lax.all_to_all(pieces, axis, 0, 0, tiled=True, axis_index_groups=groups)  134 us
    all_to_all x7, starting transfers between devices, exchange(): lax.all_to_all(pieces, axis, 0, 0, tiled=True, axis_index_groups=groups)  43.8 us
    unnamed x48, local copies, waits for them, and re-layouts  31.5 us
    all_to_all x1, blocking collectives, exchange(): lax.all_to_all(pieces, axis, 0, 0, tiled=True, axis_index_groups=groups)  30.5 us
    ppermute x1, waiting for transfers between devices, shards(): four = ordered(upper, two, lax.ppermute(two, 'rep', beside))  23.1 us
    pallas_call x1, Pallas kernels, outer(): pl.pallas_call(outer_kernel, grid_spec=pltpu.PrefetchScalarGridSpec(num_s...  10.1 us
    pallas_call x1, Pallas kernels, last(): pl.pallas_call(last_kernel, grid_spec=pltpu.PrefetchScalarGridSpec(num_sc...  7.84 us
    pallas_call x2, Pallas kernels, partial_of(): pl.pallas_call(partial_kernel, grid=(2,), in_specs=[pl.BlockSpec((per, to...  7.51 us
  transfers between devices with their start and end apart: 13, of which 10 were waited for; matrix products, arithmetic and copies ran while one was open for 1% of the time, Pallas kernels for 6%

profile of v2, /device:TPU:1, one launch (start us, length us, event | category | flops | bytes accessed | tf_op | source)
XLA Modules:
  0.0 333.0 jit_solution(2426294502915133471)
XLA Ops:
  7.2 2.2 copy-done.5
  10.9 7.5 %all-to-all-start = ((bf16[8,128,1024]{2,1,0:T(8,128)(2,1)}), bf16[8,128,1024]{2,1,0:T(8,128)(2,1)}, u32[]{:S(2)}, u32[]{:S(2)}) async-start(bf16[8,128,1024]{2,1,0:T(8,128)(2,1)} %shard_map.95), calls=%async_computation | async-start | bytes 4194304 | tf_op jit(solution)/shard_map/all_to_all | solution.py:36
  18.4 2.2 copy-done.6
  22.1 22.5 %all-to-all-done.x_ref = bf16[8,128,1024]{2,1,0:T(8,128)(2,1)} async-done(((bf16[8,128,1024]{2,1,0:T(8,128)(2,1)}), bf16[8,128,1024]{2,1,0:T(8,128)(2,1)}, u32[]{:S(2)}, u32[]{:S(2)}) %all-to-all-start) | async-done | bytes 2097184 | tf_op jit(solution)/shard_map/all_to_all | solution.py:36
  44.6 3.8 %shard_map.97 = bf16[8,128,1024]{2,1,0:T(8,128)(2,1)S(1)} custom-call(bf16[8,128,1024]{2,1,0:T(8,128)(2,1)} %all-to-all-done.x_ref, bf16[1024,1024]{1,0:T(8,128)(2,1)S(1)} %copy-done.1, bf16[8,128,1024]{2,1,0:T(8,128)(2,1)} %shard_map.96.after_ref.x_ref), custom_call_target="tpu_custom_call" | custom-call | flops 2147483648 | bytes 6291456 | tf_op jit(solution)/shard_map/pallas_call | solution.py:123
  49.7 5.3 %all-to-all-start.1 = ((bf16[8,128,1024]{2,1,0:T(8,128)(2,1)}), bf16[8,128,1024]{2,1,0:T(8,128)(2,1)}, u32[]{:S(2)}, u32[]{:S(2)}) async-start(bf16[8,128,1024]{2,1,0:T(8,128)(2,1)} %copy-done.9), calls=%async_computation.1 | async-start | bytes 4194304 | tf_op jit(solution)/shard_map/all_to_all | solution.py:36
  55.2 26.1 %all-to-all-done.1.a_ref = bf16[8,128,1024]{2,1,0:T(8,128)(2,1)} async-done(((bf16[8,128,1024]{2,1,0:T(8,128)(2,1)}), bf16[8,128,1024]{2,1,0:T(8,128)(2,1)}, u32[]{:S(2)}, u32[]{:S(2)}) %all-to-all-start.1) | async-done | bytes 2097184 | tf_op jit(solution)/shard_map/all_to_all | solution.py:36
  84.5 5.3 %all-to-all-start.2 = ((bf16[8,128,1024]{2,1,0:T(8,128)(2,1)}), bf16[8,128,1024]{2,1,0:T(8,128)(2,1)}, u32[]{:S(2)}, u32[]{:S(2)}) async-start(bf16[8,128,1024]{2,1,0:T(8,128)(2,1)} %copy-done.3), calls=%async_computation.2 | async-start | bytes 4194304 | tf_op jit(solution)/shard_map/all_to_all | solution.py:36
  94.3 23.1 %collective-permute-done.1 = bf16[2,3,32,512]{3,2,1,0:T(8,128)(2,1)S(1)} collective-permute-done((bf16[2,3,32,512]{3,2,1,0:T(8,128)(2,1)S(1)}, bf16[2,3,32,512]{3,2,1,0:T(8,128)(2,1)S(1)}, u32[]{:S(2)}, u32[]{:S(2)}) %collective-permute-start.1) | collective-permute-done | bytes 196640 | tf_op jit(solution)/shard_map/ppermute | solution.py:419
  117.5 6.9 %all-to-all-start.3 = ((bf16[8,128,1024]{2,1,0:T(8,128)(2,1)}), bf16[8,128,1024]{2,1,0:T(8,128)(2,1)}, u32[]{:S(2)}, u32[]{:S(2)}) async-start(bf16[8,128,1024]{2,1,0:T(8,128)(2,1)} %shard_map.100), calls=%async_computation.3 | async-start | bytes 4194304 | tf_op jit(solution)/shard_map/all_to_all | solution.py:36
  127.6 7.0 %shard_map.101 = (f32[1024,1024]{1,0:T(8,128)S(1)}, f32[1024,1024]{1,0:T(8,128)S(1)}, f32[1024,1024]{1,0:T(8,128)S(1)}, bf16[1024,1024]{1,0:T(8,128)(2,1)S(1)}) custom-call(bf16[8,128,1024]{2,1,0:T(8,128)(2,1)} %all-to-all-done.x_ref, bf16[8,128,1024]{2,1,0:T(8,128)(2,1)} %all-to-all-done.2.refs_0_.r_ref, bf16[1024,1024]{1,0:T(8,128)(2,1)S(1)} %copy-done.1, ...), custom_call_target="tpu_custom_call" | custom-call | flops 2147483648 | bytes 27262976 | tf_op jit(solution)/shard_map/pallas_call | solution.py:217
  135.9 2.0 copy-done.12
  137.9 2.0 copy-done.14
  139.9 2.0 copy-done.16
  141.9 8.7 %all-to-all-done.3.x_ref = bf16[8,128,1024]{2,1,0:T(8,128)(2,1)} async-done(((bf16[8,128,1024]{2,1,0:T(8,128)(2,1)}), bf16[8,128,1024]{2,1,0:T(8,128)(2,1)}, u32[]{:S(2)}, u32[]{:S(2)}) %all-to-all-start.3) | async-done | bytes 2097184 | tf_op jit(solution)/shard_map/all_to_all | solution.py:36
  152.2 3.8 %shard_map.102 = bf16[8,128,1024]{2,1,0:T(8,128)(2,1)S(1)} custom-call(bf16[8,128,1024]{2,1,0:T(8,128)(2,1)} %all-to-all-done.3.x_ref, bf16[1024,1024]{1,0:T(8,128)(2,1)S(1)} %copy-done.11, bf16[1024,1024]{1,0:T(8,128)(2,1)S(1)} %copy-done.11), custom_call_target="tpu_custom_call" | custom-call | flops 2147483648 | bytes 6291456 | tf_op jit(solution)/shard_map/pallas_call | solution.py:123
  157.3 5.2 %all-to-all-start.4 = ((bf16[8,128,1024]{2,1,0:T(8,128)(2,1)}), bf16[8,128,1024]{2,1,0:T(8,128)(2,1)}, u32[]{:S(2)}, u32[]{:S(2)}) async-start(bf16[8,128,1024]{2,1,0:T(8,128)(2,1)} %copy-done.8), calls=%async_computation.4 | async-start | bytes 4194304 | tf_op jit(solution)/shard_map/all_to_all | solution.py:36
  163.6 25.3 %all-to-all-done.4.a_ref = bf16[8,128,1024]{2,1,0:T(8,128)(2,1)} async-done(((bf16[8,128,1024]{2,1,0:T(8,128)(2,1)}), bf16[8,128,1024]{2,1,0:T(8,128)(2,1)}, u32[]{:S(2)}, u32[]{:S(2)}) %all-to-all-start.4) | async-done | bytes 2097184 | tf_op jit(solution)/shard_map/all_to_all | solution.py:36
  188.8 1.8 shard_map.103
  192.0 5.2 %all-to-all-start.5 = ((bf16[8,128,1024]{2,1,0:T(8,128)(2,1)}), bf16[8,128,1024]{2,1,0:T(8,128)(2,1)}, u32[]{:S(2)}, u32[]{:S(2)}) async-start(bf16[8,128,1024]{2,1,0:T(8,128)(2,1)} %copy-done.7), calls=%async_computation.5 | async-start | bytes 4194304 | tf_op jit(solution)/shard_map/all_to_all | solution.py:36
  197.3 26.2 %all-to-all-done.5.r_ref = bf16[8,128,1024]{2,1,0:T(8,128)(2,1)} async-done(((bf16[8,128,1024]{2,1,0:T(8,128)(2,1)}), bf16[8,128,1024]{2,1,0:T(8,128)(2,1)}, u32[]{:S(2)}, u32[]{:S(2)}) %all-to-all-start.5) | async-done | bytes 2097184 | tf_op jit(solution)/shard_map/all_to_all | solution.py:36
  223.5 2.2 copy-done.13
  225.7 2.2 copy-done.15
  227.8 2.2 copy-done.17
  230.0 7.8 %shard_map.104 = (f32[512,1024]{1,0:T(8,128)S(1)}, bf16[512,1024]{1,0:T(8,128)(2,1)S(1)}) custom-call(s32[3]{0:T(128)S(1)} %pad_add_fusion.3.place_ref, bf16[8,128,1024]{2,1,0:T(8,128)(2,1)} %all-to-all-done.3.x_ref, bf16[8,128,1024]{2,1,0:T(8,128)(2,1)} %all-to-all-done.5.r_ref, bf16[1024,1024]{1,0:T(8,128)(2,1)S(1)} %copy-done.1, ...), custom_call_target="tpu_custom_call" | custom-call | flops 2147483648 | bytes 20971520 | tf_op jit(solution)/shard_map/pallas_call | solution.py:260
  239.2 2.3 collective-permute-done.3
  242.8 8.3 %all-to-all-start.6 = ((bf16[16,32,1024]{2,1,0:T(8,128)(2,1)}), bf16[16,32,1024]{2,1,0:T(8,128)(2,1)}, u32[]{:S(2)}, u32[]{:S(2)}) async-start(bf16[16,32,1024]{2,1,0:T(8,128)(2,1)} %bitcast.14), calls=%async_computation.6 | async-start | bytes 2097152 | tf_op jit(solution)/shard_map/all_to_all | solution.py:36
  251.9 24.8 %all-to-all-done.6.a_ref = bf16[16,32,1024]{2,1,0:T(8,128)(2,1)} async-done(((bf16[16,32,1024]{2,1,0:T(8,128)(2,1)}), bf16[16,32,1024]{2,1,0:T(8,128)(2,1)}, u32[]{:S(2)}, u32[]{:S(2)}) %all-to-all-start.6) | async-done | bytes 1048608 | tf_op jit(solution)/shard_map/all_to_all | solution.py:36
  278.1 30.5 %all_to_all.40 = bf16[16,32,1024]{2,1,0:T(8,128)(2,1)} all-to-all(bf16[16,32,1024]{2,1,0:T(8,128)(2,1)S(1)} %shard_map.105), channel_id=1, replica_groups={{0,16,32,48,64,80,96,112,128,144,160,176,192,208,224,240},{8,24,40,56,7..., dimensions={0} | all-to-all | bytes 2097152 | tf_op jit(solution)/shard_map/all_to_all | solution.py:36
  308.6 3.2 collective-permute-start.4
  311.9 2.5 collective-permute-done.4.other_ref
  316.0 10.1 %shard_map.106 = (bf16[1024,1024]{1,0:T(8,128)(2,1)}, f32[32,1024]{1,0:T(8,128)}) custom-call(s32[3]{0:T(128)S(1)} %pad_add_fusion.place_ref, bf16[8,2,2,3,32,512]{5,4,3,2,1,0:T(8,128)(2,1)S(1)} %copy-done, bf16[8,2,2,3,32,512]{5,4,3,2,1,0:T(8,128)(2,1)} %collective-permute-done.2.far_left.far_low.far_high.far_mom, ...), custom_call_target="tpu_custom_call" | custom-call | flops 4294967296 | bytes 14680064 | tf_op jit(solution)/shard_map/pallas_call | solution.py:346
  (68 shorter events, 28.4 us)
Async XLA Ops:
  7.2 2.2 copy-start.5
  10.9 33.7 %all-to-all-start = ((bf16[8,128,1024]{2,1,0:T(8,128)(2,1)}), bf16[8,128,1024]{2,1,0:T(8,128)(2,1)}, u32[]{:S(2)}, u32[]{:S(2)}) async-start(bf16[8,128,1024]{2,1,0:T(8,128)(2,1)} %shard_map.95), calls=%async_computation | async-start | bytes 4194304 | tf_op jit(solution)/shard_map/all_to_all | solution.py:36
  18.4 2.2 copy-start.6
  20.6 24.1 %copy-start.1 = (bf16[1024,1024]{1,0:T(8,128)(2,1)S(1)}, bf16[1024,1024]{1,0:T(8,128)(2,1)}, u32[]{:S(2)}) copy-start(bf16[1024,1024]{1,0:T(8,128)(2,1)} %g_ref.3) | copy-start | bytes 6291460
  49.7 5.3 %copy-start.23 = (s32[1,2,128]{2,1,0:T(2,128)S(1)}, s32[1,2,128]{2,1,0:T(2,128)}, u32[]{:S(2)}) copy-start(s32[1,2,128]{2,1,0:T(2,128)} %param.12) | copy-start | bytes 3076
  49.7 31.6 %all-to-all-start.1 = ((bf16[8,128,1024]{2,1,0:T(8,128)(2,1)}), bf16[8,128,1024]{2,1,0:T(8,128)(2,1)}, u32[]{:S(2)}, u32[]{:S(2)}) async-start(bf16[8,128,1024]{2,1,0:T(8,128)(2,1)} %copy-done.9), calls=%async_computation.1 | async-start | bytes 4194304 | tf_op jit(solution)/shard_map/all_to_all | solution.py:36
  84.5 5.4 %copy-start.20 = (f32[32,1024]{1,0:T(8,128)S(1)}, f32[32,1024]{1,0:T(8,128)}, u32[]{:S(2)}) copy-start(f32[32,1024]{1,0:T(8,128)} %own_ref.1) | copy-start | bytes 393220
  84.5 5.4 %copy-start.21 = (bf16[32,1024]{1,0:T(8,128)(2,1)S(1)}, bf16[32,1024]{1,0:T(8,128)(2,1)}, u32[]{:S(2)}) copy-start(bf16[32,1024]{1,0:T(8,128)(2,1)} %refs_3_.1) | copy-start | bytes 196612
  84.5 5.4 %copy-start.22 = (bf16[1,32,1024]{2,1,0:T(8,128)(2,1)S(1)}, bf16[1,32,1024]{2,1,0:T(8,128)(2,1)}, u32[]{:S(2)}) copy-start(bf16[1,32,1024]{2,1,0:T(8,128)(2,1)} %refs_4_.1) | copy-start | bytes 196612
  84.5 33.0 %all-to-all-start.2 = ((bf16[8,128,1024]{2,1,0:T(8,128)(2,1)}), bf16[8,128,1024]{2,1,0:T(8,128)(2,1)}, u32[]{:S(2)}, u32[]{:S(2)}) async-start(bf16[8,128,1024]{2,1,0:T(8,128)(2,1)} %copy-done.3), calls=%async_computation.2 | async-start | bytes 4194304 | tf_op jit(solution)/shard_map/all_to_all | solution.py:36
  89.9 1.6 copy-start.4
  92.1 1.8 collective-permute-start
  93.9 23.6 %collective-permute-start.1 = (bf16[2,3,32,512]{3,2,1,0:T(8,128)(2,1)S(1)}, bf16[2,3,32,512]{3,2,1,0:T(8,128)(2,1)S(1)}, u32[]{:S(2)}, u32[]{:S(2)}) collective-permute-start(bf16[2,3,32,512]{3,2,1,0:T(8,128)(2,1)S(1)} %maximum_select_fusion.3), channel_id=1, source_target_pairs={{0,128},{8,136},{16,144},{24,152},{32,160},{40,168},{48,176},{56,1... | collective-permute-start | bytes 589832 | tf_op jit(solution)/shard_map/ppermute | solution.py:419
  117.5 33.1 %all-to-all-start.3 = ((bf16[8,128,1024]{2,1,0:T(8,128)(2,1)}), bf16[8,128,1024]{2,1,0:T(8,128)(2,1)}, u32[]{:S(2)}, u32[]{:S(2)}) async-start(bf16[8,128,1024]{2,1,0:T(8,128)(2,1)} %shard_map.100), calls=%async_computation.3 | async-start | bytes 4194304 | tf_op jit(solution)/shard_map/all_to_all | solution.py:36
  124.4 1.6 copy-start.18
  126.0 1.6 copy-start.19
  135.9 2.0 copy-start.12
  137.9 2.0 copy-start.14
  139.9 2.0 copy-start.16
  150.7 1.6 copy-start.11
  157.3 31.5 %all-to-all-start.4 = ((bf16[8,128,1024]{2,1,0:T(8,128)(2,1)}), bf16[8,128,1024]{2,1,0:T(8,128)(2,1)}, u32[]{:S(2)}, u32[]{:S(2)}) async-start(bf16[8,128,1024]{2,1,0:T(8,128)(2,1)} %copy-done.8), calls=%async_computation.4 | async-start | bytes 4194304 | tf_op jit(solution)/shard_map/all_to_all | solution.py:36
  162.5 88.6 %all-gather.2.cloned.1.call-start = ((), (), s32[]{:S(2)}) async-start(), calls=%async_computation.8 | async-start | bytes 3538944 | tf_op jit(solution)/shard_map/all_gather | solution.py:420
  192.0 31.5 %all-to-all-start.5 = ((bf16[8,128,1024]{2,1,0:T(8,128)(2,1)}), bf16[8,128,1024]{2,1,0:T(8,128)(2,1)}, u32[]{:S(2)}, u32[]{:S(2)}) async-start(bf16[8,128,1024]{2,1,0:T(8,128)(2,1)} %copy-done.7), calls=%async_computation.5 | async-start | bytes 4194304 | tf_op jit(solution)/shard_map/all_to_all | solution.py:36
  223.5 2.2 copy-start.13
  225.7 2.2 copy-start.15
  227.8 2.2 copy-start.17
  237.9 3.6 %collective-permute-start.3 = (bf16[512,1024]{1,0:T(8,128)(2,1)S(1)}, bf16[512,1024]{1,0:T(8,128)(2,1)S(1)}, u32[]{:S(2)}, u32[]{:S(2)}) collective-permute-start(bf16[512,1024]{1,0:T(8,128)(2,1)S(1)} %get-tuple-element.17), channel_id=1, source_target_pairs={{0,8},{8,0},{16,24},{24,16},{32,40},{40,32},{48,56},{56,48},{64,72... | collective-permute-start | bytes 3145736 | tf_op jit(solution)/shard_map/ppermute | solution.py:426
  242.8 33.9 %all-to-all-start.6 = ((bf16[16,32,1024]{2,1,0:T(8,128)(2,1)}), bf16[16,32,1024]{2,1,0:T(8,128)(2,1)}, u32[]{:S(2)}, u32[]{:S(2)}) async-start(bf16[16,32,1024]{2,1,0:T(8,128)(2,1)} %bitcast.14), calls=%async_computation.6 | async-start | bytes 2097152 | tf_op jit(solution)/shard_map/all_to_all | solution.py:36
  251.2 63.3 %copy-start = (bf16[8,2,2,3,32,512]{5,4,3,2,1,0:T(8,128)(2,1)S(1)}, bf16[8,2,2,3,32,512]{5,4,3,2,1,0:T(8,128)(2,1)}, u32[]{:S(2)}) copy-start(bf16[8,2,2,3,32,512]{5,4,3,2,1,0:T(8,128)(2,1)} %all-gather.2.cloned.1.call-done.near_left.near_low.near_high.near_mom) | copy-start | bytes 9437188
  251.2 60.7 %collective-permute-start.2 = (bf16[8,2,2,3,32,512]{5,4,3,2,1,0:T(8,128)(2,1)}, bf16[8,2,2,3,32,512]{5,4,3,2,1,0:T(8,128)(2,1)}, u32[]{:S(2)}, u32[]{:S(2)}) collective-permute-start(bf16[8,2,2,3,32,512]{5,4,3,2,1,0:T(8,128)(2,1)} %all-gather.2.cloned.1.call-done.near_left.near_low.near_high.near_mom), channel_id=1, source_target_pairs={{0,8},{8,0},{16,24},{24,16},{32,40},{40,32},{48,56},{56,48},{64,72... | collective-permute-start | bytes 9437192 | tf_op jit(solution)/shard_map/ppermute | solution.py:421
  308.6 5.8 %collective-permute-start.4 = (bf16[512,1024]{1,0:T(8,128)(2,1)}, bf16[512,1024]{1,0:T(8,128)(2,1)}, u32[]{:S(2)}, u32[]{:S(2)}) collective-permute-start(bf16[512,1024]{1,0:T(8,128)(2,1)} %bitcast.15.mine_ref), channel_id=1, source_target_pairs={{0,8},{8,0},{16,24},{24,16},{32,40},{40,32},{48,56},{56,48},{64,72... | collective-permute-start | bytes 3145736 | tf_op jit(solution)/shard_map/ppermute | solution.py:429
  314.4 1.6 copy-start.2
  (5 other events, 6.6 us)
Sparse Core Ops, SparseCore 0:
  165.2 48.0 all-gather.1

commit v3 on v2

--- a/solution.py
+++ b/solution.py
@@ -32,6 +32,10 @@
     return pl.CostEstimate(flops=flops, bytes_accessed=size, transcendentals=0)
 
 
+def apart(x):
+    return pltpu.with_memory_space_constraint(x, pltpu.HBM)
+
+
 def exchange(pieces, axis, groups=None):
     return lax.all_to_all(pieces, axis, 0, 0, tiled=True, axis_index_groups=groups)
 
@@ -54,7 +58,7 @@
         out_shape=jax.ShapeDtypeStruct((pieces, tokens, width), batch.dtype),
         compiler_params=params(),
         cost_estimate=cost(0, 4 * tokens * total),
-    )(batch)
+    )(apart(batch))
 
 
 def hold_kernel(x_ref, *refs):
@@ -129,7 +133,7 @@
             ANY,
         ],
         out_specs=pl.BlockSpec((per, tokens, width), lambda i: (i, 0, 0)),
-        out_shape=jax.ShapeDtypeStruct((pieces, tokens, width), bf16),
+        out_shape=pltpu.HBM((pieces, tokens, width), bf16),
         compiler_params=params(),
         cost_estimate=cost(2 * pieces * tokens * rows * width, 6 * rows * width),
     )(features, weights, after)
@@ -155,7 +159,7 @@
         grid=(2,),
         in_specs=[spec, pl.BlockSpec((tokens, 1), lambda i: (0, 0))],
         out_specs=spec,
-        out_shape=jax.ShapeDtypeStruct(arrived.shape, bf16),
+        out_shape=pltpu.HBM(arrived.shape, bf16),
         compiler_params=params(),
         cost_estimate=cost(0, 4 * arrived.size),
     )(arrived, labels)
@@ -420,8 +424,11 @@
     near = lax.all_gather(four, "rep", axis=0, axis_index_groups=column)
     far = lax.ppermute(near, "rep", swap)
     following = exchange(hold(split, residual, four), "fsdp")
-    *state, rounded = middle(features, residual, global_params, first_moment, second_moment)
-    partial = partial_of(following, rounded, rounded)
+    *state, rounded = middle(
+        features, residual, global_params, apart(first_moment), apart(second_moment)
+    )
+    state = [apart(x) for x in state]
+    partial = partial_of(following, apart(rounded), residual)
     mine, sent = last(stamp(3), following, exchange(own_residual(partial, 1), "fsdp"), global_params, state)
     pair = (mine + lax.ppermute(sent, "rep", swap).astype(f32)).astype(bf16)
     arrived = exchange(pair.reshape(chips, owned, width), "rep", same_core)

time: 334 us -> 324 us (0.970)
  local copies, waits for them, and re-layouts: 31.7 us -> 12.4 us
  Pallas kernels: 41.2 us -> 47.5 us
    unnamed x48 -> x28, local copies, waits for them, and re-layouts: 31.5 us -> 12.1 us
  transfers between devices with their start and end apart: 13 -> 13, of which waited for: 10 -> 10; matrix products, arithmetic and copies ran while one was open for 1% -> 1% of each run, Pallas kernels for 6% -> 7%
where the time goes in v3:
time: 324 us; the launch traced here: 323 us
  waiting for transfers between devices  165 us (51%)
  starting transfers between devices  50.4 us (16%)
  Pallas kernels  47.5 us (15%)
  blocking collectives  30.5 us (9%)
  between operations  14.2 us (4%)
  local copies, waits for them, and re-layouts  12.4 us (4%)
    all_to_all x7, waiting for transfers between devices, exchange(): lax.all_to_all(pieces, axis, 0, 0, tiled=True, axis_index_groups=groups)  136 us
    all_to_all x7, starting transfers between devices, exchange(): lax.all_to_all(pieces, axis, 0, 0, tiled=True, axis_index_groups=groups)  43.9 us
    all_to_all x1, blocking collectives, exchange(): lax.all_to_all(pieces, axis, 0, 0, tiled=True, axis_index_groups=groups)  30.5 us
    ppermute x1, waiting for transfers between devices, shards(): four = ordered(upper, two, lax.ppermute(two, 'rep', beside))  23 us
    unnamed x28, local copies, waits for them, and re-layouts  12.1 us
    pallas_call x2, Pallas kernels, partial_of(): pl.pallas_call(partial_kernel, grid=(2,), in_specs=[pl.BlockSpec((per, to...  10.1 us
    pallas_call x1, Pallas kernels, outer(): pl.pallas_call(outer_kernel, grid_spec=pltpu.PrefetchScalarGridSpec(num_s...  10.1 us
    pallas_call x1, Pallas kernels, last(): pl.pallas_call(last_kernel, grid_spec=pltpu.PrefetchScalarGridSpec(num_sc...  9.94 us
  transfers between devices with their start and end apart: 13, of which 10 were waited for; matrix products, arithmetic and copies ran while one was open for 1% of the time, Pallas kernels for 7%

profile of v3, /device:TPU:1, one launch (start us, length us, event | category | flops | bytes accessed | tf_op | source)
XLA Modules:
  0.0 322.7 jit_solution(13198073481841595546)
XLA Ops:
  7.2 2.6 shard_map.95
  9.8 7.5 %all-to-all-start = ((bf16[8,128,1024]{2,1,0:T(8,128)(2,1)}), bf16[8,128,1024]{2,1,0:T(8,128)(2,1)}, u32[]{:S(2)}, u32[]{:S(2)}) async-start(bf16[8,128,1024]{2,1,0:T(8,128)(2,1)} %shard_map.95), calls=%async_computation | async-start | bytes 4194304 | tf_op jit(solution)/shard_map/all_to_all | solution.py:40
  17.3 2.8 shard_map.96.after_ref.x_ref
  20.0 23.5 %all-to-all-done.x_ref = bf16[8,128,1024]{2,1,0:T(8,128)(2,1)} async-done(((bf16[8,128,1024]{2,1,0:T(8,128)(2,1)}), bf16[8,128,1024]{2,1,0:T(8,128)(2,1)}, u32[]{:S(2)}, u32[]{:S(2)}) %all-to-all-start) | async-done | bytes 2097184 | tf_op jit(solution)/shard_map/all_to_all | solution.py:40
  43.5 4.7 %shard_map.97 = bf16[8,128,1024]{2,1,0:T(8,128)(2,1)} custom-call(bf16[8,128,1024]{2,1,0:T(8,128)(2,1)} %all-to-all-done.x_ref, bf16[1024,1024]{1,0:T(8,128)(2,1)S(1)} %copy-done.1, bf16[8,128,1024]{2,1,0:T(8,128)(2,1)} %shard_map.96.after_ref.x_ref), custom_call_target="tpu_custom_call" | custom-call | flops 2147483648 | bytes 6291456 | tf_op jit(solution)/shard_map/pallas_call | solution.py:127
  48.2 5.3 %all-to-all-start.1 = ((bf16[8,128,1024]{2,1,0:T(8,128)(2,1)}), bf16[8,128,1024]{2,1,0:T(8,128)(2,1)S(1)}, u32[]{:S(2)}, u32[]{:S(2)}) async-start(bf16[8,128,1024]{2,1,0:T(8,128)(2,1)} %shard_map.97), calls=%async_computation.1 | async-start | bytes 4194304 | tf_op jit(solution)/shard_map/all_to_all | solution.py:40
  53.7 26.0 %all-to-all-done.1.a_ref = bf16[8,128,1024]{2,1,0:T(8,128)(2,1)S(1)} async-done(((bf16[8,128,1024]{2,1,0:T(8,128)(2,1)}), bf16[8,128,1024]{2,1,0:T(8,128)(2,1)S(1)}, u32[]{:S(2)}, u32[]{:S(2)}) %all-to-all-start.1) | async-done | bytes 2097184 | tf_op jit(solution)/shard_map/all_to_all | solution.py:40
  79.7 1.7 shard_map.98.refs_6_
  81.4 5.3 %all-to-all-start.2 = ((bf16[8,128,1024]{2,1,0:T(8,128)(2,1)}), bf16[8,128,1024]{2,1,0:T(8,128)(2,1)S(1)}, u32[]{:S(2)}, u32[]{:S(2)}) async-start(bf16[8,128,1024]{2,1,0:T(8,128)(2,1)} %shard_map.98.refs_6_), calls=%async_computation.2 | async-start | bytes 4194304 | tf_op jit(solution)/shard_map/all_to_all | solution.py:40
  91.2 23.0 %collective-permute-done.1 = bf16[2,3,32,512]{3,2,1,0:T(8,128)(2,1)S(1)} collective-permute-done((bf16[2,3,32,512]{3,2,1,0:T(8,128)(2,1)S(1)}, bf16[2,3,32,512]{3,2,1,0:T(8,128)(2,1)S(1)}, u32[]{:S(2)}, u32[]{:S(2)}) %collective-permute-start.1) | collective-permute-done | bytes 196640 | tf_op jit(solution)/shard_map/ppermute | solution.py:423
  114.3 7.0 %all-to-all-start.3 = ((bf16[8,128,1024]{2,1,0:T(8,128)(2,1)}), bf16[8,128,1024]{2,1,0:T(8,128)(2,1)}, u32[]{:S(2)}, u32[]{:S(2)}) async-start(bf16[8,128,1024]{2,1,0:T(8,128)(2,1)} %shard_map.100), calls=%async_computation.3 | async-start | bytes 4194304 | tf_op jit(solution)/shard_map/all_to_all | solution.py:40
  121.3 1.6 copy-done.2
  122.9 6.6 %shard_map.101 = (f32[1024,1024]{1,0:T(8,128)S(1)}, f32[1024,1024]{1,0:T(8,128)S(1)}, f32[1024,1024]{1,0:T(8,128)S(1)}, bf16[1024,1024]{1,0:T(8,128)(2,1)S(1)}) custom-call(bf16[8,128,1024]{2,1,0:T(8,128)(2,1)} %all-to-all-done.x_ref, bf16[8,128,1024]{2,1,0:T(8,128)(2,1)S(1)} %all-to-all-done.2.refs_0_.r_ref.after_ref, bf16[1024,1024]{1,0:T(8,128)(2,1)S(1)} %copy-done.2, ...), custom_call_target="tpu_custom_call" | custom-call | flops 2147483648 | bytes 27262976 | tf_op jit(solution)/shard_map/pallas_call | solution.py:221
  129.6 2.0 copy-done.6
  131.5 2.0 copy-done.7
  133.6 2.0 copy-done.8
  136.9 10.7 %all-to-all-done.3.x_ref = bf16[8,128,1024]{2,1,0:T(8,128)(2,1)} async-done(((bf16[8,128,1024]{2,1,0:T(8,128)(2,1)}), bf16[8,128,1024]{2,1,0:T(8,128)(2,1)}, u32[]{:S(2)}, u32[]{:S(2)}) %all-to-all-start.3) | async-done | bytes 2097184 | tf_op jit(solution)/shard_map/all_to_all | solution.py:40
  147.6 5.4 %shard_map.102 = bf16[8,128,1024]{2,1,0:T(8,128)(2,1)} custom-call(bf16[8,128,1024]{2,1,0:T(8,128)(2,1)} %all-to-all-done.3.x_ref, bf16[1024,1024]{1,0:T(8,128)(2,1)} %copy-done.9, bf16[8,128,1024]{2,1,0:T(8,128)(2,1)S(1)} %all-to-all-done.2.refs_0_.r_ref.after_ref), custom_call_target="tpu_custom_call" | custom-call | flops 2147483648 | bytes 6291456 | tf_op jit(solution)/shard_map/pallas_call | solution.py:127
  153.0 5.2 %all-to-all-start.4 = ((bf16[8,128,1024]{2,1,0:T(8,128)(2,1)}), bf16[8,128,1024]{2,1,0:T(8,128)(2,1)S(1)}, u32[]{:S(2)}, u32[]{:S(2)}) async-start(bf16[8,128,1024]{2,1,0:T(8,128)(2,1)} %shard_map.102), calls=%async_computation.4 | async-start | bytes 4194304 | tf_op jit(solution)/shard_map/all_to_all | solution.py:40
  159.2 25.2 %all-to-all-done.4.a_ref = bf16[8,128,1024]{2,1,0:T(8,128)(2,1)S(1)} async-done(((bf16[8,128,1024]{2,1,0:T(8,128)(2,1)}), bf16[8,128,1024]{2,1,0:T(8,128)(2,1)S(1)}, u32[]{:S(2)}, u32[]{:S(2)}) %all-to-all-start.4) | async-done | bytes 2097184 | tf_op jit(solution)/shard_map/all_to_all | solution.py:40
  184.5 1.7 shard_map.103
  186.1 5.2 %all-to-all-start.5 = ((bf16[8,128,1024]{2,1,0:T(8,128)(2,1)}), bf16[8,128,1024]{2,1,0:T(8,128)(2,1)}, u32[]{:S(2)}, u32[]{:S(2)}) async-start(bf16[8,128,1024]{2,1,0:T(8,128)(2,1)} %shard_map.103), calls=%async_computation.5 | async-start | bytes 4194304 | tf_op jit(solution)/shard_map/all_to_all | solution.py:40
  191.4 26.2 %all-to-all-done.5.r_ref = bf16[8,128,1024]{2,1,0:T(8,128)(2,1)} async-done(((bf16[8,128,1024]{2,1,0:T(8,128)(2,1)}), bf16[8,128,1024]{2,1,0:T(8,128)(2,1)}, u32[]{:S(2)}, u32[]{:S(2)}) %all-to-all-start.5) | async-done | bytes 2097184 | tf_op jit(solution)/shard_map/all_to_all | solution.py:40
  217.6 9.9 %shard_map.104 = (f32[512,1024]{1,0:T(8,128)S(1)}, bf16[512,1024]{1,0:T(8,128)(2,1)S(1)}) custom-call(s32[3]{0:T(128)S(1)} %pad_add_fusion.3.place_ref, bf16[8,128,1024]{2,1,0:T(8,128)(2,1)} %all-to-all-done.3.x_ref, bf16[8,128,1024]{2,1,0:T(8,128)(2,1)} %all-to-all-done.5.r_ref, bf16[1024,1024]{1,0:T(8,128)(2,1)S(1)} %copy-done.3, f32[1024,1024]{1,0:T(8,128)} %copy-done.6, ...), custom_call_target="tpu_custom_call" | custom-call | flops 2147483648 | bytes 20971520 | tf_op jit(solution)/shard_map/pallas_call | solution.py:264
  228.9 2.3 collective-permute-done.3
  232.5 8.3 %all-to-all-start.6 = ((bf16[16,32,1024]{2,1,0:T(8,128)(2,1)}), bf16[16,32,1024]{2,1,0:T(8,128)(2,1)}, u32[]{:S(2)}, u32[]{:S(2)}) async-start(bf16[16,32,1024]{2,1,0:T(8,128)(2,1)} %bitcast.14), calls=%async_computation.6 | async-start | bytes 2097152 | tf_op jit(solution)/shard_map/all_to_all | solution.py:40
  241.6 24.8 %all-to-all-done.6.a_ref = bf16[16,32,1024]{2,1,0:T(8,128)(2,1)} async-done(((bf16[16,32,1024]{2,1,0:T(8,128)(2,1)}), bf16[16,32,1024]{2,1,0:T(8,128)(2,1)}, u32[]{:S(2)}, u32[]{:S(2)}) %all-to-all-start.6) | async-done | bytes 1048608 | tf_op jit(solution)/shard_map/all_to_all | solution.py:40
  267.8 30.5 %all_to_all.40 = bf16[16,32,1024]{2,1,0:T(8,128)(2,1)} all-to-all(bf16[16,32,1024]{2,1,0:T(8,128)(2,1)S(1)} %shard_map.105), channel_id=1, replica_groups={{0,16,32,48,64,80,96,112,128,144,160,176,192,208,224,240},{8,24,40,56,7..., dimensions={0} | all-to-all | bytes 2097152 | tf_op jit(solution)/shard_map/all_to_all | solution.py:40
  298.4 3.2 collective-permute-start.4
  301.6 2.5 collective-permute-done.4.other_ref
  304.1 1.6 copy-done.4
  305.7 10.1 %shard_map.106 = (bf16[1024,1024]{1,0:T(8,128)(2,1)}, f32[32,1024]{1,0:T(8,128)}) custom-call(s32[3]{0:T(128)S(1)} %pad_add_fusion.place_ref, bf16[8,2,2,3,32,512]{5,4,3,2,1,0:T(8,128)(2,1)S(1)} %copy-done, bf16[8,2,2,3,32,512]{5,4,3,2,1,0:T(8,128)(2,1)} %collective-permute-done.2.far_left.far_low.far_high.far_mom, ...), custom_call_target="tpu_custom_call" | custom-call | flops 4294967296 | bytes 14680064 | tf_op jit(solution)/shard_map/pallas_call | solution.py:350
  (48 shorter events, 12.0 us)
Async XLA Ops:
  9.8 33.7 %all-to-all-start = ((bf16[8,128,1024]{2,1,0:T(8,128)(2,1)}), bf16[8,128,1024]{2,1,0:T(8,128)(2,1)}, u32[]{:S(2)}, u32[]{:S(2)}) async-start(bf16[8,128,1024]{2,1,0:T(8,128)(2,1)} %shard_map.95), calls=%async_computation | async-start | bytes 4194304 | tf_op jit(solution)/shard_map/all_to_all | solution.py:40
  17.3 26.3 %copy-start.1 = (bf16[1024,1024]{1,0:T(8,128)(2,1)S(1)}, bf16[1024,1024]{1,0:T(8,128)(2,1)}, u32[]{:S(2)}) copy-start(bf16[1024,1024]{1,0:T(8,128)(2,1)} %g_ref.3) | copy-start | bytes 6291460
  48.2 5.3 %copy-start.13 = (s32[1,2,128]{2,1,0:T(2,128)S(1)}, s32[1,2,128]{2,1,0:T(2,128)}, u32[]{:S(2)}) copy-start(s32[1,2,128]{2,1,0:T(2,128)} %param.12) | copy-start | bytes 3076
  48.2 31.5 %all-to-all-start.1 = ((bf16[8,128,1024]{2,1,0:T(8,128)(2,1)}), bf16[8,128,1024]{2,1,0:T(8,128)(2,1)S(1)}, u32[]{:S(2)}, u32[]{:S(2)}) async-start(bf16[8,128,1024]{2,1,0:T(8,128)(2,1)} %shard_map.97), calls=%async_computation.1 | async-start | bytes 4194304 | tf_op jit(solution)/shard_map/all_to_all | solution.py:40
  81.4 5.4 %copy-start.10 = (f32[32,1024]{1,0:T(8,128)S(1)}, f32[32,1024]{1,0:T(8,128)}, u32[]{:S(2)}) copy-start(f32[32,1024]{1,0:T(8,128)} %own_ref.1) | copy-start | bytes 393220
  81.4 5.4 %copy-start.11 = (bf16[32,1024]{1,0:T(8,128)(2,1)S(1)}, bf16[32,1024]{1,0:T(8,128)(2,1)}, u32[]{:S(2)}) copy-start(bf16[32,1024]{1,0:T(8,128)(2,1)} %refs_3_.1) | copy-start | bytes 196612
  81.4 5.4 %copy-start.12 = (bf16[1,32,1024]{2,1,0:T(8,128)(2,1)S(1)}, bf16[1,32,1024]{2,1,0:T(8,128)(2,1)}, u32[]{:S(2)}) copy-start(bf16[1,32,1024]{2,1,0:T(8,128)(2,1)} %refs_4_.1) | copy-start | bytes 196612
  81.4 32.9 %all-to-all-start.2 = ((bf16[8,128,1024]{2,1,0:T(8,128)(2,1)}), bf16[8,128,1024]{2,1,0:T(8,128)(2,1)S(1)}, u32[]{:S(2)}, u32[]{:S(2)}) async-start(bf16[8,128,1024]{2,1,0:T(8,128)(2,1)} %shard_map.98.refs_6_), calls=%async_computation.2 | async-start | bytes 4194304 | tf_op jit(solution)/shard_map/all_to_all | solution.py:40
  86.8 1.6 copy-start.5
  89.0 1.8 collective-permute-start
  90.8 23.5 %collective-permute-start.1 = (bf16[2,3,32,512]{3,2,1,0:T(8,128)(2,1)S(1)}, bf16[2,3,32,512]{3,2,1,0:T(8,128)(2,1)S(1)}, u32[]{:S(2)}, u32[]{:S(2)}) collective-permute-start(bf16[2,3,32,512]{3,2,1,0:T(8,128)(2,1)S(1)} %maximum_select_fusion.3), channel_id=1, source_target_pairs={{0,128},{8,136},{16,144},{24,152},{32,160},{40,168},{48,176},{56,1... | collective-permute-start | bytes 589832 | tf_op jit(solution)/shard_map/ppermute | solution.py:423
  114.3 33.2 %all-to-all-start.3 = ((bf16[8,128,1024]{2,1,0:T(8,128)(2,1)}), bf16[8,128,1024]{2,1,0:T(8,128)(2,1)}, u32[]{:S(2)}, u32[]{:S(2)}) async-start(bf16[8,128,1024]{2,1,0:T(8,128)(2,1)} %shard_map.100), calls=%async_computation.3 | async-start | bytes 4194304 | tf_op jit(solution)/shard_map/all_to_all | solution.py:40
  121.3 1.6 copy-start.2
  129.6 2.0 copy-start.6
  131.5 2.0 copy-start.7
  133.6 2.0 copy-start.8
  135.6 1.3 copy-start.9
  153.0 31.5 %all-to-all-start.4 = ((bf16[8,128,1024]{2,1,0:T(8,128)(2,1)}), bf16[8,128,1024]{2,1,0:T(8,128)(2,1)S(1)}, u32[]{:S(2)}, u32[]{:S(2)}) async-start(bf16[8,128,1024]{2,1,0:T(8,128)(2,1)} %shard_map.102), calls=%async_computation.4 | async-start | bytes 4194304 | tf_op jit(solution)/shard_map/all_to_all | solution.py:40
  158.2 82.7 %all-gather.2.cloned.1.call-start = ((), (), s32[]{:S(2)}) async-start(), calls=%async_computation.8 | async-start | bytes 3538944 | tf_op jit(solution)/shard_map/all_gather | solution.py:424
  186.1 31.5 %copy-start.3 = (bf16[1024,1024]{1,0:T(8,128)(2,1)S(1)}, bf16[1024,1024]{1,0:T(8,128)(2,1)}, u32[]{:S(2)}) copy-start(bf16[1024,1024]{1,0:T(8,128)(2,1)} %g_ref.3) | copy-start | bytes 6291460
  186.1 31.5 %all-to-all-start.5 = ((bf16[8,128,1024]{2,1,0:T(8,128)(2,1)}), bf16[8,128,1024]{2,1,0:T(8,128)(2,1)}, u32[]{:S(2)}, u32[]{:S(2)}) async-start(bf16[8,128,1024]{2,1,0:T(8,128)(2,1)} %shard_map.103), calls=%async_computation.5 | async-start | bytes 4194304 | tf_op jit(solution)/shard_map/all_to_all | solution.py:40
  227.6 3.6 %collective-permute-start.3 = (bf16[512,1024]{1,0:T(8,128)(2,1)S(1)}, bf16[512,1024]{1,0:T(8,128)(2,1)S(1)}, u32[]{:S(2)}, u32[]{:S(2)}) collective-permute-start(bf16[512,1024]{1,0:T(8,128)(2,1)S(1)} %get-tuple-element.17), channel_id=1, source_target_pairs={{0,8},{8,0},{16,24},{24,16},{32,40},{40,32},{48,56},{56,48},{64,72... | collective-permute-start | bytes 3145736 | tf_op jit(solution)/shard_map/ppermute | solution.py:433
  232.5 33.9 %all-to-all-start.6 = ((bf16[16,32,1024]{2,1,0:T(8,128)(2,1)}), bf16[16,32,1024]{2,1,0:T(8,128)(2,1)}, u32[]{:S(2)}, u32[]{:S(2)}) async-start(bf16[16,32,1024]{2,1,0:T(8,128)(2,1)} %bitcast.14), calls=%async_computation.6 | async-start | bytes 2097152 | tf_op jit(solution)/shard_map/all_to_all | solution.py:40
  240.9 63.3 %copy-start = (bf16[8,2,2,3,32,512]{5,4,3,2,1,0:T(8,128)(2,1)S(1)}, bf16[8,2,2,3,32,512]{5,4,3,2,1,0:T(8,128)(2,1)}, u32[]{:S(2)}) copy-start(bf16[8,2,2,3,32,512]{5,4,3,2,1,0:T(8,128)(2,1)} %all-gather.2.cloned.1.call-done.near_left.near_low.near_high.near_mom) | copy-start | bytes 9437188
  240.9 60.7 %collective-permute-start.2 = (bf16[8,2,2,3,32,512]{5,4,3,2,1,0:T(8,128)(2,1)}, bf16[8,2,2,3,32,512]{5,4,3,2,1,0:T(8,128)(2,1)}, u32[]{:S(2)}, u32[]{:S(2)}) collective-permute-start(bf16[8,2,2,3,32,512]{5,4,3,2,1,0:T(8,128)(2,1)} %all-gather.2.cloned.1.call-done.near_left.near_low.near_high.near_mom), channel_id=1, source_target_pairs={{0,8},{8,0},{16,24},{24,16},{32,40},{40,32},{48,56},{56,48},{64,72... | collective-permute-start | bytes 9437192 | tf_op jit(solution)/shard_map/ppermute | solution.py:425
  298.4 5.8 %collective-permute-start.4 = (bf16[512,1024]{1,0:T(8,128)(2,1)}, bf16[512,1024]{1,0:T(8,128)(2,1)}, u32[]{:S(2)}, u32[]{:S(2)}) collective-permute-start(bf16[512,1024]{1,0:T(8,128)(2,1)} %bitcast.15.mine_ref), channel_id=1, source_target_pairs={{0,8},{8,0},{16,24},{24,16},{32,40},{40,32},{48,56},{56,48},{64,72... | collective-permute-start | bytes 3145736 | tf_op jit(solution)/shard_map/ppermute | solution.py:436
  304.1 1.6 copy-start.4
Sparse Core Ops, SparseCore 0:
  160.8 48.0 all-gather.1

commit v4 on v3

--- a/solution.py
+++ b/solution.py
@@ -9,7 +9,7 @@
 
 INNER = 2
 BLOCK = 256
-SCOPED = 28 * 1024 * 1024
+SCOPED = 22 * 1024 * 1024
 
 inner_rate = 0.01
 beta_one = 0.9
@@ -331,6 +331,7 @@
 def outer(place, near, far, mine, other, start, momentum):
     depth, _, cores, _, owned, half = near.shape
     width = mine.shape[1]
+    near, far = apart(near), apart(far)
 
     def piece(what, row):
         return pl.BlockSpec(
@@ -378,7 +379,7 @@
         ],
         compiler_params=params(),
         cost_estimate=cost(4 * width**3, 14 * width * width),
-    )(place, near, far, near, near, far, far, near, far, mine, other, start, momentum)
+    )(place, near, far, near, near, far, far, near, far, mine, other, apart(start), momentum)
 
 
 def shards(

time: 324 us -> 321 us (level)
    unnamed x28 -> x24, local copies, waits for them, and re-layouts: 12.1 us -> 10.5 us
where the time goes in v4:
time: 321 us; the launch traced here: 320 us
  waiting for transfers between devices  165 us (51%)
  starting transfers between devices  50.4 us (16%)
  Pallas kernels  46.8 us (15%)
  blocking collectives  30.4 us (9%)
  between operations  14.2 us (4%)
  local copies, waits for them, and re-layouts  10.7 us (3%)
    all_to_all x7, waiting for transfers between devices, exchange(): lax.all_to_all(pieces, axis, 0, 0, tiled=True, axis_index_groups=groups)  136 us
    all_to_all x7, starting transfers between devices, exchange(): lax.all_to_all(pieces, axis, 0, 0, tiled=True, axis_index_groups=groups)  43.9 us
    all_to_all x1, blocking collectives, exchange(): lax.all_to_all(pieces, axis, 0, 0, tiled=True, axis_index_groups=groups)  30.4 us
    ppermute x1, waiting for transfers between devices, shards(): four = ordered(upper, two, lax.ppermute(two, 'rep', beside))  23 us
    pallas_call x1, Pallas kernels, outer(): pl.pallas_call(outer_kernel, grid_spec=pltpu.PrefetchScalarGridSpec(num_s...  10.6 us
    unnamed x24, local copies, waits for them, and re-layouts  10.5 us
    pallas_call x2, Pallas kernels, partial_of(): pl.pallas_call(partial_kernel, grid=(2,), in_specs=[pl.BlockSpec((per, to...  10.2 us
    pallas_call x1, Pallas kernels, last(): pl.pallas_call(last_kernel, grid_spec=pltpu.PrefetchScalarGridSpec(num_sc...  9.93 us
  transfers between devices with their start and end apart: 13, of which 10 were waited for; matrix products, arithmetic and copies ran while one was open for 1% of the time, Pallas kernels for 7%

profile of v4, /device:TPU:1, one launch (start us, length us, event | category | flops | bytes accessed | tf_op | source)
XLA Modules:
  0.0 319.9 jit_solution(13382402584897920061)
XLA Ops:
  7.2 2.6 shard_map.95
  9.8 7.5 %all-to-all-start = ((bf16[8,128,1024]{2,1,0:T(8,128)(2,1)}), bf16[8,128,1024]{2,1,0:T(8,128)(2,1)}, u32[]{:S(2)}, u32[]{:S(2)}) async-start(bf16[8,128,1024]{2,1,0:T(8,128)(2,1)} %shard_map.95), calls=%async_computation | async-start | bytes 4194304 | tf_op jit(solution)/shard_map/all_to_all | solution.py:40
  17.3 2.8 shard_map.96.after_ref.x_ref
  20.0 23.5 %all-to-all-done.x_ref = bf16[8,128,1024]{2,1,0:T(8,128)(2,1)} async-done(((bf16[8,128,1024]{2,1,0:T(8,128)(2,1)}), bf16[8,128,1024]{2,1,0:T(8,128)(2,1)}, u32[]{:S(2)}, u32[]{:S(2)}) %all-to-all-start) | async-done | bytes 2097184 | tf_op jit(solution)/shard_map/all_to_all | solution.py:40
  43.5 4.7 %shard_map.97 = bf16[8,128,1024]{2,1,0:T(8,128)(2,1)} custom-call(bf16[8,128,1024]{2,1,0:T(8,128)(2,1)} %all-to-all-done.x_ref, bf16[1024,1024]{1,0:T(8,128)(2,1)S(1)} %copy-done, bf16[8,128,1024]{2,1,0:T(8,128)(2,1)} %shard_map.96.after_ref.x_ref), custom_call_target="tpu_custom_call" | custom-call | flops 2147483648 | bytes 6291456 | tf_op jit(solution)/shard_map/pallas_call | solution.py:127
  48.2 5.3 %all-to-all-start.1 = ((bf16[8,128,1024]{2,1,0:T(8,128)(2,1)}), bf16[8,128,1024]{2,1,0:T(8,128)(2,1)S(1)}, u32[]{:S(2)}, u32[]{:S(2)}) async-start(bf16[8,128,1024]{2,1,0:T(8,128)(2,1)} %shard_map.97), calls=%async_computation.1 | async-start | bytes 4194304 | tf_op jit(solution)/shard_map/all_to_all | solution.py:40
  53.7 26.0 %all-to-all-done.1.a_ref = bf16[8,128,1024]{2,1,0:T(8,128)(2,1)S(1)} async-done(((bf16[8,128,1024]{2,1,0:T(8,128)(2,1)}), bf16[8,128,1024]{2,1,0:T(8,128)(2,1)S(1)}, u32[]{:S(2)}, u32[]{:S(2)}) %all-to-all-start.1) | async-done | bytes 2097184 | tf_op jit(solution)/shard_map/all_to_all | solution.py:40
  79.7 1.7 shard_map.98.refs_6_
  81.4 5.3 %all-to-all-start.2 = ((bf16[8,128,1024]{2,1,0:T(8,128)(2,1)}), bf16[8,128,1024]{2,1,0:T(8,128)(2,1)S(1)}, u32[]{:S(2)}, u32[]{:S(2)}) async-start(bf16[8,128,1024]{2,1,0:T(8,128)(2,1)} %shard_map.98.refs_6_), calls=%async_computation.2 | async-start | bytes 4194304 | tf_op jit(solution)/shard_map/all_to_all | solution.py:40
  86.8 1.6 copy-done.3
  91.2 23.0 %collective-permute-done.1 = bf16[2,3,32,512]{3,2,1,0:T(8,128)(2,1)S(1)} collective-permute-done((bf16[2,3,32,512]{3,2,1,0:T(8,128)(2,1)S(1)}, bf16[2,3,32,512]{3,2,1,0:T(8,128)(2,1)S(1)}, u32[]{:S(2)}, u32[]{:S(2)}) %collective-permute-start.1) | collective-permute-done | bytes 196640 | tf_op jit(solution)/shard_map/ppermute | solution.py:424
  114.3 7.0 %all-to-all-start.3 = ((bf16[8,128,1024]{2,1,0:T(8,128)(2,1)}), bf16[8,128,1024]{2,1,0:T(8,128)(2,1)}, u32[]{:S(2)}, u32[]{:S(2)}) async-start(bf16[8,128,1024]{2,1,0:T(8,128)(2,1)} %shard_map.100), calls=%async_computation.3 | async-start | bytes 4194304 | tf_op jit(solution)/shard_map/all_to_all | solution.py:40
  121.3 1.6 copy-done.1
  122.9 6.6 %shard_map.101 = (f32[1024,1024]{1,0:T(8,128)S(1)}, f32[1024,1024]{1,0:T(8,128)S(1)}, f32[1024,1024]{1,0:T(8,128)S(1)}, bf16[1024,1024]{1,0:T(8,128)(2,1)S(1)}) custom-call(bf16[8,128,1024]{2,1,0:T(8,128)(2,1)} %all-to-all-done.x_ref, bf16[8,128,1024]{2,1,0:T(8,128)(2,1)S(1)} %all-to-all-done.2.refs_0_.r_ref.after_ref, bf16[1024,1024]{1,0:T(8,128)(2,1)S(1)} %copy-done.1, ...), custom_call_target="tpu_custom_call" | custom-call | flops 2147483648 | bytes 27262976 | tf_op jit(solution)/shard_map/pallas_call | solution.py:221
  129.6 2.0 copy-done.4
  131.5 2.0 copy-done.5
  133.6 2.0 copy-done.6
  136.9 10.7 %all-to-all-done.3.x_ref = bf16[8,128,1024]{2,1,0:T(8,128)(2,1)} async-done(((bf16[8,128,1024]{2,1,0:T(8,128)(2,1)}), bf16[8,128,1024]{2,1,0:T(8,128)(2,1)}, u32[]{:S(2)}, u32[]{:S(2)}) %all-to-all-start.3) | async-done | bytes 2097184 | tf_op jit(solution)/shard_map/all_to_all | solution.py:40
  147.6 5.5 %shard_map.102 = bf16[8,128,1024]{2,1,0:T(8,128)(2,1)} custom-call(bf16[8,128,1024]{2,1,0:T(8,128)(2,1)} %all-to-all-done.3.x_ref, bf16[1024,1024]{1,0:T(8,128)(2,1)} %copy-done.7, bf16[8,128,1024]{2,1,0:T(8,128)(2,1)S(1)} %all-to-all-done.2.refs_0_.r_ref.after_ref), custom_call_target="tpu_custom_call" | custom-call | flops 2147483648 | bytes 6291456 | tf_op jit(solution)/shard_map/pallas_call | solution.py:127
  153.0 5.2 %all-to-all-start.4 = ((bf16[8,128,1024]{2,1,0:T(8,128)(2,1)}), bf16[8,128,1024]{2,1,0:T(8,128)(2,1)S(1)}, u32[]{:S(2)}, u32[]{:S(2)}) async-start(bf16[8,128,1024]{2,1,0:T(8,128)(2,1)} %shard_map.102), calls=%async_computation.4 | async-start | bytes 4194304 | tf_op jit(solution)/shard_map/all_to_all | solution.py:40
  159.3 25.3 %all-to-all-done.4.a_ref = bf16[8,128,1024]{2,1,0:T(8,128)(2,1)S(1)} async-done(((bf16[8,128,1024]{2,1,0:T(8,128)(2,1)}), bf16[8,128,1024]{2,1,0:T(8,128)(2,1)S(1)}, u32[]{:S(2)}, u32[]{:S(2)}) %all-to-all-start.4) | async-done | bytes 2097184 | tf_op jit(solution)/shard_map/all_to_all | solution.py:40
  184.5 1.7 shard_map.103
  186.2 5.2 %all-to-all-start.5 = ((bf16[8,128,1024]{2,1,0:T(8,128)(2,1)}), bf16[8,128,1024]{2,1,0:T(8,128)(2,1)}, u32[]{:S(2)}, u32[]{:S(2)}) async-start(bf16[8,128,1024]{2,1,0:T(8,128)(2,1)} %shard_map.103), calls=%async_computation.5 | async-start | bytes 4194304 | tf_op jit(solution)/shard_map/all_to_all | solution.py:40
  191.5 26.2 %all-to-all-done.5.r_ref = bf16[8,128,1024]{2,1,0:T(8,128)(2,1)} async-done(((bf16[8,128,1024]{2,1,0:T(8,128)(2,1)}), bf16[8,128,1024]{2,1,0:T(8,128)(2,1)}, u32[]{:S(2)}, u32[]{:S(2)}) %all-to-all-start.5) | async-done | bytes 2097184 | tf_op jit(solution)/shard_map/all_to_all | solution.py:40
  217.7 9.9 %shard_map.104 = (f32[512,1024]{1,0:T(8,128)S(1)}, bf16[512,1024]{1,0:T(8,128)(2,1)S(1)}) custom-call(s32[3]{0:T(128)S(1)} %pad_add_fusion.3.place_ref, bf16[8,128,1024]{2,1,0:T(8,128)(2,1)} %all-to-all-done.3.x_ref, bf16[8,128,1024]{2,1,0:T(8,128)(2,1)} %all-to-all-done.5.r_ref, bf16[1024,1024]{1,0:T(8,128)(2,1)S(1)} %copy-done.2, f32[1024,1024]{1,0:T(8,128)} %copy-done.4, ...), custom_call_target="tpu_custom_call" | custom-call | flops 2147483648 | bytes 20971520 | tf_op jit(solution)/shard_map/pallas_call | solution.py:264
  228.9 2.3 collective-permute-done.3
  232.5 8.3 %all-to-all-start.6 = ((bf16[16,32,1024]{2,1,0:T(8,128)(2,1)}), bf16[16,32,1024]{2,1,0:T(8,128)(2,1)S(1)}, u32[]{:S(2)}, u32[]{:S(2)}) async-start(bf16[16,32,1024]{2,1,0:T(8,128)(2,1)} %bitcast.14), calls=%async_computation.6 | async-start | bytes 2097152 | tf_op jit(solution)/shard_map/all_to_all | solution.py:40
  241.6 24.8 %all-to-all-done.6.a_ref = bf16[16,32,1024]{2,1,0:T(8,128)(2,1)S(1)} async-done(((bf16[16,32,1024]{2,1,0:T(8,128)(2,1)}), bf16[16,32,1024]{2,1,0:T(8,128)(2,1)S(1)}, u32[]{:S(2)}, u32[]{:S(2)}) %all-to-all-start.6) | async-done | bytes 1048608 | tf_op jit(solution)/shard_map/all_to_all | solution.py:40
  266.6 30.4 %all_to_all.40 = bf16[16,32,1024]{2,1,0:T(8,128)(2,1)S(1)} all-to-all(bf16[16,32,1024]{2,1,0:T(8,128)(2,1)S(1)} %shard_map.105), channel_id=1, replica_groups={{0,16,32,48,64,80,96,112,128,144,160,176,192,208,224,240},{8,24,40,56,7..., dimensions={0} | all-to-all | bytes 2097152 | tf_op jit(solution)/shard_map/all_to_all | solution.py:40
  297.0 3.2 collective-permute-start.4
  300.2 2.2 collective-permute-done.4.other_ref
  302.4 10.6 %shard_map.106 = (bf16[1024,1024]{1,0:T(8,128)(2,1)}, f32[32,1024]{1,0:T(8,128)}) custom-call(s32[3]{0:T(128)S(1)} %pad_add_fusion.place_ref, bf16[8,2,2,3,32,512]{5,4,3,2,1,0:T(8,128)(2,1)} %all-gather.2.cloned.1.call-done.near_left.near_low.near_high.near_mom, bf16[8,2,2,3,32,512]{5,4,3,2,1,0:T(8,128)(2,1)} %collective-permute-done.2.far_left.far_low.far_high.far_mom, ...), custom_call_target="tpu_custom_call" | custom-call | flops 4294967296 | bytes 14680064 | tf_op jit(solution)/shard_map/pallas_call | solution.py:351
  (44 shorter events, 9.1 us)
Async XLA Ops:
  9.8 33.7 %all-to-all-start = ((bf16[8,128,1024]{2,1,0:T(8,128)(2,1)}), bf16[8,128,1024]{2,1,0:T(8,128)(2,1)}, u32[]{:S(2)}, u32[]{:S(2)}) async-start(bf16[8,128,1024]{2,1,0:T(8,128)(2,1)} %shard_map.95), calls=%async_computation | async-start | bytes 4194304 | tf_op jit(solution)/shard_map/all_to_all | solution.py:40
  17.3 26.3 %copy-start = (bf16[1024,1024]{1,0:T(8,128)(2,1)S(1)}, bf16[1024,1024]{1,0:T(8,128)(2,1)}, u32[]{:S(2)}) copy-start(bf16[1024,1024]{1,0:T(8,128)(2,1)} %g_ref.3) | copy-start | bytes 6291460
  48.2 5.3 %copy-start.11 = (s32[1,2,128]{2,1,0:T(2,128)S(1)}, s32[1,2,128]{2,1,0:T(2,128)}, u32[]{:S(2)}) copy-start(s32[1,2,128]{2,1,0:T(2,128)} %param.12) | copy-start | bytes 3076
  48.2 31.5 %all-to-all-start.1 = ((bf16[8,128,1024]{2,1,0:T(8,128)(2,1)}), bf16[8,128,1024]{2,1,0:T(8,128)(2,1)S(1)}, u32[]{:S(2)}, u32[]{:S(2)}) async-start(bf16[8,128,1024]{2,1,0:T(8,128)(2,1)} %shard_map.97), calls=%async_computation.1 | async-start | bytes 4194304 | tf_op jit(solution)/shard_map/all_to_all | solution.py:40
  81.4 5.4 %copy-start.8 = (f32[32,1024]{1,0:T(8,128)S(1)}, f32[32,1024]{1,0:T(8,128)}, u32[]{:S(2)}) copy-start(f32[32,1024]{1,0:T(8,128)} %own_ref.1) | copy-start | bytes 393220
  81.4 5.4 %copy-start.9 = (bf16[32,1024]{1,0:T(8,128)(2,1)S(1)}, bf16[32,1024]{1,0:T(8,128)(2,1)}, u32[]{:S(2)}) copy-start(bf16[32,1024]{1,0:T(8,128)(2,1)} %refs_3_.1) | copy-start | bytes 196612
  81.4 5.4 %copy-start.10 = (bf16[1,32,1024]{2,1,0:T(8,128)(2,1)S(1)}, bf16[1,32,1024]{2,1,0:T(8,128)(2,1)}, u32[]{:S(2)}) copy-start(bf16[1,32,1024]{2,1,0:T(8,128)(2,1)} %refs_4_.1) | copy-start | bytes 196612
  81.4 32.9 %all-to-all-start.2 = ((bf16[8,128,1024]{2,1,0:T(8,128)(2,1)}), bf16[8,128,1024]{2,1,0:T(8,128)(2,1)S(1)}, u32[]{:S(2)}, u32[]{:S(2)}) async-start(bf16[8,128,1024]{2,1,0:T(8,128)(2,1)} %shard_map.98.refs_6_), calls=%async_computation.2 | async-start | bytes 4194304 | tf_op jit(solution)/shard_map/all_to_all | solution.py:40
  86.8 1.6 copy-start.3
  89.0 1.8 collective-permute-start
  90.8 23.5 %collective-permute-start.1 = (bf16[2,3,32,512]{3,2,1,0:T(8,128)(2,1)S(1)}, bf16[2,3,32,512]{3,2,1,0:T(8,128)(2,1)S(1)}, u32[]{:S(2)}, u32[]{:S(2)}) collective-permute-start(bf16[2,3,32,512]{3,2,1,0:T(8,128)(2,1)S(1)} %maximum_select_fusion.3), channel_id=1, source_target_pairs={{0,128},{8,136},{16,144},{24,152},{32,160},{40,168},{48,176},{56,1... | collective-permute-start | bytes 589832 | tf_op jit(solution)/shard_map/ppermute | solution.py:424
  114.3 33.2 %all-to-all-start.3 = ((bf16[8,128,1024]{2,1,0:T(8,128)(2,1)}), bf16[8,128,1024]{2,1,0:T(8,128)(2,1)}, u32[]{:S(2)}, u32[]{:S(2)}) async-start(bf16[8,128,1024]{2,1,0:T(8,128)(2,1)} %shard_map.100), calls=%async_computation.3 | async-start | bytes 4194304 | tf_op jit(solution)/shard_map/all_to_all | solution.py:40
  121.3 1.6 copy-start.1
  129.6 2.0 copy-start.4
  131.5 2.0 copy-start.5
  133.6 2.0 copy-start.6
  135.6 1.3 copy-start.7
  153.0 31.5 %all-to-all-start.4 = ((bf16[8,128,1024]{2,1,0:T(8,128)(2,1)}), bf16[8,128,1024]{2,1,0:T(8,128)(2,1)S(1)}, u32[]{:S(2)}, u32[]{:S(2)}) async-start(bf16[8,128,1024]{2,1,0:T(8,128)(2,1)} %shard_map.102), calls=%async_computation.4 | async-start | bytes 4194304 | tf_op jit(solution)/shard_map/all_to_all | solution.py:40
  158.2 82.6 %all-gather.2.cloned.1.call-start = ((), (), s32[]{:S(2)}) async-start(), calls=%async_computation.8 | async-start | bytes 3538944 | tf_op jit(solution)/shard_map/all_gather | solution.py:425
  186.2 31.5 %copy-start.2 = (bf16[1024,1024]{1,0:T(8,128)(2,1)S(1)}, bf16[1024,1024]{1,0:T(8,128)(2,1)}, u32[]{:S(2)}) copy-start(bf16[1024,1024]{1,0:T(8,128)(2,1)} %g_ref.3) | copy-start | bytes 6291460
  186.2 31.5 %all-to-all-start.5 = ((bf16[8,128,1024]{2,1,0:T(8,128)(2,1)}), bf16[8,128,1024]{2,1,0:T(8,128)(2,1)}, u32[]{:S(2)}, u32[]{:S(2)}) async-start(bf16[8,128,1024]{2,1,0:T(8,128)(2,1)} %shard_map.103), calls=%async_computation.5 | async-start | bytes 4194304 | tf_op jit(solution)/shard_map/all_to_all | solution.py:40
  227.6 3.6 %collective-permute-start.3 = (bf16[512,1024]{1,0:T(8,128)(2,1)S(1)}, bf16[512,1024]{1,0:T(8,128)(2,1)S(1)}, u32[]{:S(2)}, u32[]{:S(2)}) collective-permute-start(bf16[512,1024]{1,0:T(8,128)(2,1)S(1)} %get-tuple-element.17), channel_id=1, source_target_pairs={{0,8},{8,0},{16,24},{24,16},{32,40},{40,32},{48,56},{56,48},{64,72... | collective-permute-start | bytes 3145736 | tf_op jit(solution)/shard_map/ppermute | solution.py:434
  232.5 33.8 %all-to-all-start.6 = ((bf16[16,32,1024]{2,1,0:T(8,128)(2,1)}), bf16[16,32,1024]{2,1,0:T(8,128)(2,1)S(1)}, u32[]{:S(2)}, u32[]{:S(2)}) async-start(bf16[16,32,1024]{2,1,0:T(8,128)(2,1)} %bitcast.14), calls=%async_computation.6 | async-start | bytes 2097152 | tf_op jit(solution)/shard_map/all_to_all | solution.py:40
  240.9 59.3 %collective-permute-start.2 = (bf16[8,2,2,3,32,512]{5,4,3,2,1,0:T(8,128)(2,1)}, bf16[8,2,2,3,32,512]{5,4,3,2,1,0:T(8,128)(2,1)}, u32[]{:S(2)}, u32[]{:S(2)}) collective-permute-start(bf16[8,2,2,3,32,512]{5,4,3,2,1,0:T(8,128)(2,1)} %all-gather.2.cloned.1.call-done.near_left.near_low.near_high.near_mom), channel_id=1, source_target_pairs={{0,8},{8,0},{16,24},{24,16},{32,40},{40,32},{48,56},{56,48},{64,72... | collective-permute-start | bytes 9437192 | tf_op jit(solution)/shard_map/ppermute | solution.py:426
  297.0 5.4 %collective-permute-start.4 = (bf16[512,1024]{1,0:T(8,128)(2,1)S(1)}, bf16[512,1024]{1,0:T(8,128)(2,1)S(1)}, u32[]{:S(2)}, u32[]{:S(2)}) collective-permute-start(bf16[512,1024]{1,0:T(8,128)(2,1)S(1)} %bitcast.19), channel_id=1, source_target_pairs={{0,8},{8,0},{16,24},{24,16},{32,40},{40,32},{48,56},{56,48},{64,72... | collective-permute-start | bytes 3145736 | tf_op jit(solution)/shard_map/ppermute | solution.py:437
Sparse Core Ops, SparseCore 0:
  160.9 48.0 all-gather.1
